TPU v7x, 32 devices: a whole 2x2x4 slice. The times are simulated.
32 devices in a mesh: fsdp: 4 (over y, x), ctx: 2 (over core), tp: 4 (over z).
Axes of the slice: x: 2, y: 2, z: 4, core: 2. Of those that a mesh axis runs over, the one named last changes fastest.
Arguments:
- tokens: bfloat16 [12, 640, 1024], P('fsdp', 'ctx')
- lengths: int32 [12, 2], P('fsdp'), may hold values from 257 to 320, as said below
- image_count: int32 [4], P('fsdp'), may hold values from 1 to 3, as said below
- qkv_weight: bfloat16 [2, 1024, 3, 1024], P(None, 'fsdp', None, 'tp')
- qv_bias: bfloat16 [2, 2, 4, 256], P(None, None, 'tp', 'fsdp'), may hold values from -0.59765625 to 0.59765625
- out_weight: bfloat16 [2, 1024, 1024], P(None, 'tp', 'fsdp')
- out_bias: bfloat16 [2, 1024], P(None, 'fsdp'), may hold values from -1.796875 to 1.796875
- up_weight: bfloat16 [2, 1024, 4096], P(None, 'fsdp', 'tp')
- up_bias: bfloat16 [2, 4, 1024], P(None, 'tp', 'fsdp'), may hold values from -1.796875 to 1.796875
- down_weight: bfloat16 [2, 4096, 1024], P(None, 'tp', 'fsdp')
- down_bias: bfloat16 [2, 1024], P(None, 'fsdp'), may hold values from -1.796875 to 1.796875
- gain_one: bfloat16 [2, 1024], P(None, 'fsdp'), may hold values from 0.5 to 1.5
- gain_two: bfloat16 [2, 1024], P(None, 'fsdp'), may hold values from 0.5 to 1.5
- cotangent: bfloat16 [12, 640, 1024], P('fsdp', 'ctx')
Outputs:
- output: bfloat16 [12, 640, 1024], P('fsdp', 'ctx')
- input_grad: bfloat16 [12, 640, 1024], P('fsdp', 'ctx')
- qkv_weight_grad: float32 [2, 1024, 3, 1024], P(None, 'fsdp', None, 'tp')
- qv_bias_grad: float32 [2, 2, 4, 256], P(None, None, 'tp', 'fsdp')
- out_weight_grad: float32 [2, 1024, 1024], P(None, 'tp', 'fsdp')
- out_bias_grad: float32 [2, 1024], P(None, 'fsdp')
- up_weight_grad: float32 [2, 1024, 4096], P(None, 'fsdp', 'tp')
- up_bias_grad: float32 [2, 4, 1024], P(None, 'tp', 'fsdp')
- down_weight_grad: float32 [2, 4096, 1024], P(None, 'tp', 'fsdp')
- down_bias_grad: float32 [2, 1024], P(None, 'fsdp')
- gain_one_grad: float32 [2, 1024], P(None, 'fsdp')
- gain_two_grad: float32 [2, 1024], P(None, 'fsdp')
Inputs may be any that keep to these rules, and one draw needn't show every extreme that they name: `lengths`: in each image one index of ctx, drawn from the seed, holds exactly 320 tokens; the other indices share the remaining 577 - 320 tokens as evenly as possible; each image's counts sum to 577. Slots 0 to image_count - 1 of an fsdp index hold images; some index holds 3.
All inputs are finite; a program needn't handle non-finite values.
Results may differ from a plain program's by a relative error of at most 0.02.
Values may be sent and summed in bfloat16 or wider, within the bound.
No kernel may reach another device: no remote copies, remote signals or barrier semaphores. Data moves between devices by JAX's collectives and lax.ppermute only.
A program may use at most 192 MiB of HBM per device.

v0:
```python
import jax
import jax.numpy as jnp
from jax import lax
from jax.sharding import PartitionSpec as P

HD = 64
SEQ = 577
BF = jnp.bfloat16
F32 = jnp.float32


def layer_norm(vectors, scaling):
    centre = vectors - jnp.mean(vectors, axis=-1, keepdims=True)
    spread = jnp.mean(centre * centre, axis=-1, keepdims=True)
    return centre * lax.rsqrt(spread + 1e-06) * scaling


def gelu_exact(values):
    return 0.5 * values * (1.0 + lax.erf(values * 0.7071067811865476))


X_PAIRS = [(0, 1), (1, 0), (2, 3), (3, 2)]
Y_PAIRS = [(0, 2), (2, 0), (1, 3), (3, 1)]


def square():
    return lax.axis_size("fsdp") == 4


def reorder(values):
    if not square():
        return values
    place = lax.axis_index("fsdp")
    lead = values.shape[:-1]
    blocks = values.reshape(lead + (2, 2, values.shape[-1] // 4))
    blocks = jnp.where(place % 2 == 1, blocks[..., :, ::-1, :], blocks)
    blocks = jnp.where(place >= 2, blocks[..., ::-1, :, :], blocks)
    return blocks.reshape(values.shape)


def send_x(values):
    return lax.ppermute(values, "fsdp", X_PAIRS)


def send_y(values):
    return lax.ppermute(values, "fsdp", Y_PAIRS)


def swap(values):
    return lax.ppermute(values, "ctx", [(0, 1), (1, 0)])


def both_cores(partial_sum):
    low = partial_sum.astype(BF)
    return low.astype(F32) + swap(low).astype(F32)


def gather_rows(shard):
    if not square():
        return lax.all_gather(shard, "fsdp", axis=0, tiled=True)
    half = shard.shape[0] // 2
    from_x, from_y = (send_x(shard), send_y(shard))
    far_a, far_b = (send_y(from_x[:half]), send_x(from_y[half:]))
    return jnp.concatenate([shard, from_x, from_y, far_a, far_b], axis=0)


def scatter_rows(full):
    if not square():
        return lax.psum_scatter(full.astype(BF), "fsdp", scatter_dimension=0, tiled=True).astype(
            F32
        )
    rows = full.shape[0] // 4
    half = rows // 2
    own, to_x, to_y, far = [full[k * rows : (k + 1) * rows] for k in range(4)]
    first = send_x(jnp.concatenate([to_x[:half], far[:half]]).astype(BF)).astype(F32)
    second = send_y(jnp.concatenate([to_y[half:], far[half:]]).astype(BF)).astype(F32)
    own_a = own[:half] + first[:half]
    own_b = own[half:] + second[:half]
    pass_y = (to_y[:half] + first[half:]).astype(BF)
    pass_x = (to_x[half:] + second[half:]).astype(BF)
    own_a = own_a + send_y(pass_y).astype(F32)
    own_b = own_b + send_x(pass_x).astype(F32)
    return jnp.concatenate([own_a, own_b])


def gather_matrix(shard, place):
    rows, groups, columns = shard.shape
    half = lax.dynamic_index_in_dim(
        shard.reshape(rows, groups, 2, columns // 2), place, 2, keepdims=False
    )
    along = lax.all_gather(half, "tp", axis=0)
    along = jnp.transpose(along, (1, 2, 0, 3)).reshape(rows, -1)
    return gather_rows(along)


def scatter_matrix(grad, groups, place):
    count = lax.axis_size("tp")
    kept = scatter_rows(grad).astype(BF)
    rows = kept.shape[0]
    kept = jnp.transpose(kept.reshape(rows, groups, count, -1), (2, 0, 1, 3))
    own = lax.psum_scatter(kept, "tp", scatter_dimension=0, tiled=False)
    other = swap(own)
    low = jnp.where(place == 0, own, other)
    high = jnp.where(place == 0, other, own)
    return jnp.concatenate([low, high], axis=-1).astype(F32)


def heads_of(values):
    return values.reshape(values.shape[0], -1, HD)


def masked_scores(queries, keys, key_valid):
    scores = jnp.einsum("qhd,khd->hqk", queries, keys, preferred_element_type=F32) * HD ** (-0.5)
    return jnp.where(key_valid, scores, -1000000000.0)


def mm(left, right):
    return jnp.dot(left, right, preferred_element_type=F32)


def mm_nt(left, right):
    return lax.dot_general(left, right, (((1,), (1,)), ((), ())), preferred_element_type=F32)


def mm_tn(left, right):
    return lax.dot_general(left, right, (((0,), (0,)), ((), ())), preferred_element_type=F32)


def forward_layer(stream, weights, vectors, key_valid):
    qkv, out, up, down = weights
    shift_q, shift_v, out_shift, up_shift, down_shift, gain_first, gain_second = vectors
    normed = layer_norm(stream, gain_first).astype(BF)
    project = mm(normed, qkv)
    width = project.shape[1] // 3
    queries = heads_of((project[:, :width] + shift_q).astype(BF))
    keys = heads_of(project[:, width : 2 * width].astype(BF))
    values = heads_of((project[:, 2 * width :] + shift_v).astype(BF))
    scores = masked_scores(queries, keys, key_valid)
    highest = jnp.max(scores, axis=-1, keepdims=True)
    exponent = jnp.exp(scores - highest)
    denominator = jnp.sum(exponent, axis=-1, keepdims=True)
    probs = (exponent / denominator).astype(BF)
    log_total = highest + jnp.log(denominator)
    mixed = jnp.einsum("hqk,khd->qhd", probs, values, preferred_element_type=F32).astype(BF)
    mixed = mixed.reshape(stream.shape[0], width)
    middle = stream + both_cores(mm_nt(mixed, out)) + out_shift
    normed_b = layer_norm(middle, gain_second).astype(BF)
    hidden = mm(normed_b, up) + up_shift
    active = gelu_exact(hidden).astype(BF)
    following = middle + both_cores(mm_nt(active, down)) + down_shift
    return (
        following,
        (stream, normed, queries, keys, values, log_total, mixed, middle, normed_b, hidden, active),
    )


def backward_layer(gradient, saved, weights, vectors, key_valid, emit):
    qkv, out, up, down = weights
    gain_first, gain_second = vectors[5:]
    stream, normed, queries, keys, values, log_total, mixed, middle, normed_b, hidden, active = (
        saved
    )
    total = lambda array: jnp.sum(array.astype(F32), axis=0)
    grad_low = gradient.astype(BF)
    emit("down", mm_tn(grad_low, active))
    delta_hidden = jax.vjp(gelu_exact, hidden)[1](mm(grad_low, down))[0].astype(BF)
    emit("up", mm_tn(normed_b, delta_hidden))
    delta_normed_b = both_cores(mm_nt(delta_hidden, up))
    back_middle, delta_gain_second = jax.vjp(layer_norm, middle, gain_second)[1](delta_normed_b)
    grad_middle = gradient + back_middle
    grad_attend = grad_middle.astype(BF)
    emit("out", mm_tn(grad_attend, mixed))
    delta_mixed = heads_of(mm(grad_attend, out).astype(BF))
    probs = jnp.exp(masked_scores(queries, keys, key_valid) - log_total)
    delta_values = jnp.einsum(
        "hqk,qhd->khd", probs.astype(BF), delta_mixed, preferred_element_type=F32
    ).astype(BF)
    delta_probs = jnp.einsum("qhd,khd->hqk", delta_mixed, values, preferred_element_type=F32)
    inner = jnp.sum(probs * delta_probs, axis=-1, keepdims=True)
    delta_scores = (probs * (delta_probs - inner)).astype(BF)
    scale = HD ** (-0.5)
    delta_queries = (
        jnp.einsum("hqk,khd->qhd", delta_scores, keys, preferred_element_type=F32) * scale
    ).astype(BF)
    delta_keys = (
        jnp.einsum("hqk,qhd->khd", delta_scores, queries, preferred_element_type=F32) * scale
    ).astype(BF)
    flat = [
        piece.reshape(stream.shape[0], -1) for piece in (delta_queries, delta_keys, delta_values)
    ]
    delta_project = jnp.concatenate(flat, axis=1)
    emit("qkv", mm_tn(normed, delta_project))
    delta_normed = both_cores(mm_nt(delta_project, qkv))
    back_stream, delta_gain_first = jax.vjp(layer_norm, stream, gain_first)[1](delta_normed)
    sums = (
        total(flat[0]),
        total(flat[2]),
        total(grad_attend),
        total(delta_hidden),
        total(grad_low),
        delta_gain_first,
        delta_gain_second,
    )
    return (grad_middle + back_stream, sums)


def shards(
    tokens,
    lengths,
    image_count,
    qkv_weight,
    qv_bias,
    out_weight,
    out_bias,
    up_weight,
    up_bias,
    down_weight,
    down_bias,
    gain_one,
    gain_two,
    cotangent,
):
    slots, capacity, features = tokens.shape
    layers = qkv_weight.shape[0]
    n_fsdp, n_tp = (lax.axis_size("fsdp"), lax.axis_size("tp"))
    assert lax.axis_size("ctx") == 2 and slots <= n_tp
    group, core, lane = (lax.axis_index("fsdp"), lax.axis_index("ctx"), lax.axis_index("tp"))
    rows = -(-SEQ // 16) * 16
    slot = jnp.minimum(lane, slots - 1)
    own_lengths = lax.dynamic_index_in_dim(lengths, slot, 0, keepdims=False)
    live = lane < jnp.minimum(image_count[0], slots)
    key_valid = (jnp.arange(rows) < SEQ)[None, None, :]
    row_mask = ((jnp.arange(rows) < SEQ) & live).astype(F32)[:, None]
    pieces = (qv_bias, up_bias, out_bias, down_bias, gain_one, gain_two)
    packed = jnp.concatenate([piece.reshape(-1) for piece in pieces])
    spread = lax.all_gather(packed, ("fsdp", "tp"), axis=0).reshape(n_fsdp, n_tp, -1)
    found, start = ([], 0)
    for piece in pieces:
        found.append(spread[:, :, start : start + piece.size])
        start += piece.size

    def by_core(array, count):
        array = array.reshape(n_fsdp, n_tp, layers, count, -1)
        array = jnp.transpose(array, (2, 3, 1, 0, 4)).reshape(layers, count, n_tp, 2, -1)
        return lax.dynamic_index_in_dim(array, core, 3, keepdims=False).reshape(layers, count, -1)

    def by_feature(array):
        array = array[:, 0].reshape(n_fsdp, layers, -1)
        return reorder(jnp.transpose(array, (1, 0, 2)).reshape(layers, features))

    qv_all, up_all = (by_core(found[0], 2), by_core(found[1], 1))
    out_all, down_all, one_all, two_all = [by_feature(array) for array in found[2:]]
    vectors = [
        (qv_all[l, 0], qv_all[l, 1], out_all[l], up_all[l, 0], down_all[l], one_all[l], two_all[l])
        for l in range(layers)
    ]
    weights = []
    for l in range(layers):
        raw = (
            qkv_weight[l],
            out_weight[l].T[:, None],
            up_weight[l][:, None],
            down_weight[l].T[:, None],
        )
        weights.append(tuple((gather_matrix(piece, core) for piece in raw)))
    own_pair = jnp.stack(
        [lax.dynamic_index_in_dim(a, slot, 0, keepdims=False) for a in (tokens, cotangent)]
    )
    other_pair = swap(own_pair)
    low = jnp.where(core == 0, own_pair, other_pair)
    high = jnp.where(core == 0, other_pair, own_pair)
    image = jnp.concatenate([low, jnp.zeros_like(low)], axis=1)
    image = lax.dynamic_update_slice_in_dim(image, high, own_lengths[0], 1)[:, :rows]
    image = reorder(image).astype(F32)
    stream = image[0]
    saved = []
    for l in range(layers):
        stream, items = forward_layer(stream, weights[l], vectors[l], key_valid)
        saved.append(items)
    own_length = own_lengths[core]
    own_rows = ((jnp.arange(capacity) < own_length) & live)[:, None]

    def give_back(values):
        values = jnp.pad(reorder(values.astype(BF)), ((0, 2 * capacity - rows), (0, 0)))
        mine = lax.dynamic_slice_in_dim(
            values, jnp.where(core == 0, 0, own_lengths[0]), capacity, 0
        )
        mine = jnp.where(own_rows, mine, jnp.zeros_like(mine))
        return lax.all_gather(mine, "tp", axis=0)[:slots]

    output = give_back(stream)
    gradient = image[1] * row_mask
    grads = {}
    sums = [None] * layers
    for l in reversed(range(layers)):

        def emit(name, grad, l=l):
            grads[name, l] = scatter_matrix(grad, 3 if name == "qkv" else 1, core)

        gradient, sums[l] = backward_layer(
            gradient, saved[l], weights[l], vectors[l], key_valid, emit
        )
    input_grad = give_back(gradient)

    def from_core(array, count):
        array = array.reshape(layers, count, n_tp, 1, -1)
        mask = (jnp.arange(2) == core)[:, None]
        return jnp.where(mask, array, 0.0).reshape(layers * count, -1)

    first = (core == 0).astype(F32)
    member = lambda k: jnp.stack([sums[l][k] for l in range(layers)])
    joined = [
        from_core(jnp.stack([member(0), member(1)], axis=1), 2),
        from_core(member(3)[:, None], 1),
    ] + [reorder(member(k)) * first for k in (2, 4, 5, 6)]
    summed = lax.psum(jnp.concatenate([a.reshape(-1) for a in joined]), ("fsdp", "ctx", "tp"))
    whole, start = ([], 0)
    for a in joined:
        whole.append(summed[start : start + a.size])
        start += a.size
    pick = lambda a, i, axis: lax.dynamic_index_in_dim(a, i, axis, keepdims=True)
    qv_grad = pick(pick(whole[0].reshape(layers, 2, n_tp, n_fsdp, -1), lane, 2), group, 3)[
        :, :, :, 0
    ]
    up_grad = pick(pick(whole[1].reshape(layers, n_tp, n_fsdp, -1), lane, 1), group, 2)[:, :, 0]
    out_shift, down_shift, one, two = [
        pick(a.reshape(layers, n_fsdp, -1), group, 1)[:, 0] for a in whole[2:]
    ]
    stacked = lambda name: jnp.stack([grads[name, l] for l in range(layers)])
    qkv_grad = stacked("qkv")
    out_grad = jnp.swapaxes(stacked("out")[:, :, 0], 1, 2)
    up_w_grad = stacked("up")[:, :, 0]
    down_grad = jnp.swapaxes(stacked("down")[:, :, 0], 1, 2)
    return (
        output,
        input_grad,
        qkv_grad,
        qv_grad,
        out_grad,
        out_shift,
        up_w_grad,
        up_grad,
        down_grad,
        down_shift,
        one,
        two,
    )


def solution(mesh):
    in_specs = (
        P("fsdp", "ctx", None),
        P("fsdp", None),
        P("fsdp"),
        P(None, "fsdp", None, "tp"),
        P(None, None, "tp", "fsdp"),
        P(None, "tp", "fsdp"),
        P(None, "fsdp"),
        P(None, "fsdp", "tp"),
        P(None, "tp", "fsdp"),
        P(None, "tp", "fsdp"),
        P(None, "fsdp"),
        P(None, "fsdp"),
        P(None, "fsdp"),
        P("fsdp", "ctx", None),
    )
    out_specs = (
        P("fsdp", "ctx", None),
        P("fsdp", "ctx", None),
        P(None, "fsdp", None, "tp"),
        P(None, None, "tp", "fsdp"),
        P(None, "tp", "fsdp"),
        P(None, "fsdp"),
        P(None, "fsdp", "tp"),
        P(None, "tp", "fsdp"),
        P(None, "tp", "fsdp"),
        P(None, "fsdp"),
        P(None, "fsdp"),
        P(None, "fsdp"),
    )
    return jax.shard_map(shards, mesh=mesh, in_specs=in_specs, out_specs=out_specs, check_vma=False)
```

profile of v0, /device:TPU:0, one launch (start us, length us, event | category | flops | bytes accessed | tf_op | source)
XLA Modules:
  0.0 1221.1 jit_solution(7200938606107575798)
XLA Ops:
  11.6 16.6 %all-gather.6 = bf16[1024,1,1,128]{0,3,2,1:T(8,128)(2,1)S(1)} all-gather(bf16[256,1,1,128]{0,3,2,1:T(8,128)(2,1)S(1)} %constant_dynamic-slice_fusion.8), channel_id=8, replica_groups=mesh['fsdp'=4,'ctx'=2,'tp'=4] {'tp'}, dimensions={0}, use_global_device_ids=true | all-gather | bytes 327680 | tf_op jit(solution)/shard_map/all_gather | solution.py:91
  31.9 16.8 %all-gather.2 = bf16[1024,1,1,128]{0,3,2,1:T(8,128)(2,1)S(1)} all-gather(bf16[256,1,1,128]{0,3,2,1:T(8,128)(2,1)S(1)} %constant_dynamic-slice_fusion.12), channel_id=4, replica_groups=mesh['fsdp'=4,'ctx'=2,'tp'=4] {'tp'}, dimensions={0}, use_global_device_ids=true | all-gather | bytes 327680 | tf_op jit(solution)/shard_map/all_gather | solution.py:91
  50.7 24.3 %all-gather.5 = bf16[1024,3,1,128]{0,3,2,1:T(8,128)(2,1)S(1)} all-gather(bf16[256,3,1,128]{0,3,2,1:T(8,128)(2,1)S(1)} %constant_dynamic-slice_fusion.9), channel_id=7, replica_groups=mesh['fsdp'=4,'ctx'=2,'tp'=4] {'tp'}, dimensions={0}, use_global_device_ids=true | all-gather | bytes 983040 | tf_op jit(solution)/shard_map/all_gather | solution.py:91
  80.7 39.9 %all-gather.11 = bf16[16,1,2816]{2,1,0:T(2,128)(2,1)S(1)} all-gather(bf16[1,1,2816]{2,1,0:T(2,128)(2,1)S(1)} %reshape.1168), channel_id=2, replica_groups=mesh['fsdp'=4,'ctx'=2,'tp'=4] {'fsdp','tp'}, dimensions={0}, use_global_device_ids=true | all-gather | bytes 95744 | tf_op jit(solution)/shard_map/all_gather | solution.py:236
  126.1 19.7 %all-gather.1 = bf16[1024,3,1,128]{0,3,2,1:T(8,128)(2,1)S(1)} all-gather(bf16[256,3,1,128]{0,3,2,1:T(8,128)(2,1)S(1)} %constant_dynamic-slice_fusion.13), channel_id=3, replica_groups=mesh['fsdp'=4,'ctx'=2,'tp'=4] {'tp'}, dimensions={0}, use_global_device_ids=true | all-gather | bytes 983040 | tf_op jit(solution)/shard_map/all_gather | solution.py:91
  173.7 6.3 collective-permute-done.25
  206.0 6.9 collective-permute-done.3
  216.1 9.5 dynamic_update_slice.3
  227.3 5.7 reshape.1095
  233.0 19.4 %rev.66 = bf16[2,592,2,2,256]{4,3,2,1,0:T(2,128)(2,1)} reverse(bf16[2,592,2,2,256]{4,3,2,1,0:T(2,128)(2,1)S(1)} %reshape.1095), dimensions={3} | reverse | bytes 4849664 | tf_op jit(solution)/shard_map/rev | solution.py:36
  257.4 5.0 fusion.120
  262.4 3.5 squeeze.95
  266.4 4.5 fusion.106
  277.8 3.6 fusion.134
  291.0 4.3 squeeze.100
  303.9 3.4 collective-permute-start.14
  326.4 27.2 %collective-permute-done.10 = bf16[256,2048]{0,1:T(8,128)(2,1)} collective-permute-done((bf16[256,2048]{0,1:T(8,128)(2,1)}, bf16[256,2048]{0,1:T(8,128)(2,1)}, u32[]{:S(2)}, u32[]{:S(2)}) %collective-permute-start.10) | collective-permute-done | bytes 1048608 | tf_op jit(solution)/shard_map/ppermute | solution.py:42
  367.7 16.9 %collective-permute-done.12 = bf16[128,2048]{0,1:T(8,128)(2,1)S(1)} collective-permute-done((bf16[128,2048]{0,1:T(8,128)(2,1)S(1)}, bf16[128,2048]{0,1:T(8,128)(2,1)S(1)}, u32[]{:S(2)}, u32[]{:S(2)}) %collective-permute-start.12) | collective-permute-done | bytes 524320 | tf_op jit(solution)/shard_map/ppermute | solution.py:46
  391.2 5.3 multiply_convert_fusion.3
  396.5 21.5 %collective-permute-done.16 = bf16[128,2048]{0,1:T(8,128)(2,1)S(1)} collective-permute-done((bf16[128,2048]{0,1:T(8,128)(2,1)S(1)}, bf16[128,2048]{0,1:T(8,128)(2,1)S(1)}, u32[]{:S(2)}, u32[]{:S(2)}) %collective-permute-start.16) | collective-permute-done | bytes 524320 | tf_op jit(solution)/shard_map/ppermute | solution.py:46
  431.0 14.1 %collective-permute-done.28 = bf16[256,2048]{0,1:T(8,128)(2,1)S(1)} collective-permute-done((bf16[256,2048]{0,1:T(8,128)(2,1)S(1)}, bf16[256,2048]{0,1:T(8,128)(2,1)S(1)}, u32[]{:S(2)}, u32[]{:S(2)}) %collective-permute-start.28) | collective-permute-done | bytes 1048608 | tf_op jit(solution)/shard_map/ppermute | solution.py:42
  461.7 3.6 fusion.135
  485.7 5.5 convert_reduce_fusion
  491.2 3.7 convolution_convert_fusion.1
  495.0 6.0 fusion.140
  505.5 6.0 fusion.142
  515.6 3.7 convolution_convert_fusion.2
  519.3 10.4 collective-permute-done.66
  534.1 17.7 %collective-permute-done.76 = bf16[256,2048]{1,0:T(8,128)(2,1)} collective-permute-done((bf16[256,2048]{1,0:T(8,128)(2,1)}, bf16[256,2048]{1,0:T(8,128)(2,1)}, u32[]{:S(2)}, u32[]{:S(2)}) %collective-permute-start.76) | collective-permute-done | bytes 1048608 | tf_op jit(solution)/shard_map/ppermute | solution.py:42
  566.8 4.2 fusion.116
  578.8 6.8 convert_reduce_fusion.6
  585.7 8.9 multiply_reduce_fusion.1
  594.6 6.2 multiply_convert_fusion.1
  607.7 5.5 fusion.136
  619.9 4.1 reshape.1124
  624.0 12.5 %rev.76 = bf16[592,2,2,256]{3,2,1,0:T(2,128)(2,1)} reverse(bf16[592,2,2,256]{3,2,1,0:T(2,128)(2,1)} %reshape.1124), dimensions={2} | reverse | bytes 2424832 | tf_op jit(solution)/shard_map/rev | solution.py:36
  641.7 3.4 fusion.50
  645.4 11.9 collective-permute-done.57
  674.1 3.7 fusion.38
  695.7 3.8 collective-permute-done.47
  713.4 6.9 convert_reduce_fusion.1
  720.4 3.7 convolution_convert_fusion
  724.1 6.7 fusion.141
  736.7 5.7 fusion.143
  751.4 11.0 collective-permute-done.61
  768.3 15.9 %collective-permute-done.71 = bf16[256,2048]{1,0:T(8,128)(2,1)} collective-permute-done((bf16[256,2048]{1,0:T(8,128)(2,1)}, bf16[256,2048]{1,0:T(8,128)(2,1)}, u32[]{:S(2)}, u32[]{:S(2)}) %collective-permute-start.71) | collective-permute-done | bytes 1048608 | tf_op jit(solution)/shard_map/ppermute | solution.py:42
  805.7 6.6 convert_reduce_fusion.7
  812.3 9.1 multiply_reduce_fusion
  821.4 6.2 multiply_convert_fusion
  834.5 6.6 fusion.137
  863.2 8.2 collective-permute-done.54
  885.5 3.6 fusion.56
  891.6 13.4 %collective-permute-done.41 = bf16[256,1536]{1,0:T(8,128)(2,1)} collective-permute-done((bf16[256,1536]{1,0:T(8,128)(2,1)}, bf16[256,1536]{1,0:T(8,128)(2,1)}, u32[]{:S(2)}, u32[]{:S(2)}) %collective-permute-start.41) | collective-permute-done | bytes 786464 | tf_op jit(solution)/shard_map/ppermute | solution.py:42
  918.0 3.9 broadcast_select_fusion.5
  921.9 4.0 reshape.1125
  933.2 4.1 fusion.113
  946.5 3.4 reshape.1134
  949.9 8.2 rev.78
  975.1 40.2 %all-reduce.5.cloned.1.call-done = f32[20480]{0:T(1024)} async-done(((f32[20480]{0:T(1024)}), f32[20480]{0:T(1024)}) %all-reduce.5.cloned.1.call-update) | async-done | bytes 81936 | tf_op jit(solution)/shard_map/psum | solution.py:316
  1016.1 30.6 %reduce-scatter.21.cloned.1.call-done = bf16[1,256,1,512]{3,1,2,0:T(8,128)(2,1)} async-done(((bf16[4,256,1,512]{3,1,2,0:T(8,128)(2,1)}), bf16[1,256,1,512]{3,1,2,0:T(8,128)(2,1)}) %reduce-scatter.21.cloned.1.call-update) | async-done | bytes 262160 | tf_op jit(solution)/shard_map/reduce_scatter | solution.py:101
  1051.8 23.6 %reduce-scatter.17.cloned.1.call-done = bf16[1,256,1,512]{3,1,2,0:T(8,128)(2,1)} async-done(((bf16[4,256,1,512]{3,1,2,0:T(8,128)(2,1)}), bf16[1,256,1,512]{3,1,2,0:T(8,128)(2,1)}) %reduce-scatter.17.cloned.1.call-update) | async-done | bytes 262160 | tf_op jit(solution)/shard_map/reduce_scatter | solution.py:101
  1075.3 24.9 %reduce-scatter.9.cloned.1.call-done = bf16[1,256,3,128]{3,1,2,0:T(8,128)(2,1)} async-done(((bf16[4,256,3,128]{3,1,2,0:T(8,128)(2,1)}), bf16[1,256,3,128]{3,1,2,0:T(8,128)(2,1)}) %reduce-scatter.9.cloned.1.call-update) | async-done | bytes 196624 | tf_op jit(solution)/shard_map/reduce_scatter | solution.py:101
  1108.3 48.1 %all-gather.29.cloned.1.call-done = bf16[1280,1024]{1,0:T(8,128)(2,1)} async-done(((bf16[320,1024]{1,0:T(8,128)(2,1)}), bf16[1280,1024]{1,0:T(8,128)(2,1)}) %all-gather.29.cloned.1.call-update) | async-done | bytes 2621456 | tf_op jit(solution)/shard_map/all_gather | solution.py:289
  1159.3 52.1 %all-gather.27.cloned.1.call-done = bf16[1280,1024]{1,0:T(8,128)(2,1)} async-done(((bf16[320,1024]{1,0:T(8,128)(2,1)}), bf16[1280,1024]{1,0:T(8,128)(2,1)}) %all-gather.27.cloned.1.call-update) | async-done | bytes 2621456 | tf_op jit(solution)/shard_map/all_gather | solution.py:289
  (865 shorter events, 452.1 us)
Async XLA Ops:
  7.2 292.3 %all-gather.21.cloned.1.call-start = ((), (), s32[]{:S(2)}) async-start(), calls=%async_computation.18 | async-start | bytes 1310720 | tf_op jit(solution)/shard_map/all_gather | solution.py:91
  9.4 297.9 %all-gather.19.cloned.1.call-start = ((), (), s32[]{:S(2)}) async-start(), calls=%async_computation.17 | async-start | bytes 1310720 | tf_op jit(solution)/shard_map/all_gather | solution.py:91
  10.5 300.2 %all-gather.23.cloned.1.call-start = ((), (), s32[]{:S(2)}) async-start(), calls=%async_computation.19 | async-start | bytes 1310720 | tf_op jit(solution)/shard_map/all_gather | solution.py:91
  11.5 302.9 %all-gather.25.cloned.1.call-start = ((), (), s32[]{:S(2)}) async-start(), calls=%async_computation.20 | async-start | bytes 1310720 | tf_op jit(solution)/shard_map/all_gather | solution.py:91
  28.6 124.0 %collective-permute-start.24 = (bf16[256,512]{0,1:T(8,128)(2,1)S(1)}, bf16[256,512]{0,1:T(8,128)(2,1)}, u32[]{:S(2)}, u32[]{:S(2)}) collective-permute-start(bf16[256,512]{0,1:T(8,128)(2,1)S(1)} %bitcast.413), channel_id=1, source_target_pairs={{0,16},{16,0},{8,24},{24,8},{1,17},{17,1},{9,25},{25,9},{2,18},{18... | collective-permute-start | bytes 786440 | tf_op jit(solution)/shard_map/ppermute | solution.py:46
  30.3 132.3 %collective-permute-start.23 = (bf16[256,512]{0,1:T(8,128)(2,1)S(1)}, bf16[256,512]{0,1:T(8,128)(2,1)}, u32[]{:S(2)}, u32[]{:S(2)}) collective-permute-start(bf16[256,512]{0,1:T(8,128)(2,1)S(1)} %bitcast.414), channel_id=1, source_target_pairs={{0,8},{8,0},{16,24},{24,16},{1,9},{9,1},{17,25},{25,17},{2,10},{10... | collective-permute-start | bytes 786440 | tf_op jit(solution)/shard_map/ppermute | solution.py:42
  49.0 116.7 %collective-permute-start.6 = (bf16[256,512]{0,1:T(8,128)(2,1)S(1)}, bf16[256,512]{0,1:T(8,128)(2,1)}, u32[]{:S(2)}, u32[]{:S(2)}) collective-permute-start(bf16[256,512]{0,1:T(8,128)(2,1)S(1)} %bitcast.410), channel_id=1, source_target_pairs={{0,16},{16,0},{8,24},{24,8},{1,17},{17,1},{9,25},{25,9},{2,18},{18... | collective-permute-start | bytes 786440 | tf_op jit(solution)/shard_map/ppermute | solution.py:46
  49.6 119.0 %collective-permute-start.5 = (bf16[256,512]{0,1:T(8,128)(2,1)S(1)}, bf16[256,512]{0,1:T(8,128)(2,1)}, u32[]{:S(2)}, u32[]{:S(2)}) collective-permute-start(bf16[256,512]{0,1:T(8,128)(2,1)S(1)} %bitcast.411), channel_id=1, source_target_pairs={{0,8},{8,0},{16,24},{24,16},{1,9},{9,1},{17,25},{25,17},{2,10},{10... | collective-permute-start | bytes 786440 | tf_op jit(solution)/shard_map/ppermute | solution.py:42
  75.6 115.4 %collective-permute-start.20 = (bf16[256,1536]{0,1:T(8,128)(2,1)S(1)}, bf16[256,1536]{0,1:T(8,128)(2,1)}, u32[]{:S(2)}, u32[]{:S(2)}) collective-permute-start(bf16[256,1536]{0,1:T(8,128)(2,1)S(1)} %bitcast.384), channel_id=1, source_target_pairs={{0,16},{16,0},{8,24},{24,8},{1,17},{17,1},{9,25},{25,9},{2,18},{18... | collective-permute-start | bytes 2359304 | tf_op jit(solution)/shard_map/ppermute | solution.py:46
  77.8 889.3 %reduce-scatter.15.cloned.1.call-start = ((), (), s32[]{:S(2)}) async-start(), calls=%async_computation.12 | async-start | bytes 327680 | tf_op jit(solution)/shard_map/reduce_scatter | solution.py:101
  162.6 30.5 %collective-permute-start.19 = (bf16[256,1536]{0,1:T(8,128)(2,1)S(1)}, bf16[256,1536]{0,1:T(8,128)(2,1)S(1)}, u32[]{:S(2)}, u32[]{:S(2)}) collective-permute-start(bf16[256,1536]{0,1:T(8,128)(2,1)S(1)} %bitcast.386), channel_id=1, source_target_pairs={{0,8},{8,0},{16,24},{24,16},{1,9},{9,1},{17,25},{25,17},{2,10},{10... | collective-permute-start | bytes 2359304 | tf_op jit(solution)/shard_map/ppermute | solution.py:42
  165.6 29.0 %collective-permute-start.2 = (bf16[256,1536]{0,1:T(8,128)(2,1)S(1)}, bf16[256,1536]{0,1:T(8,128)(2,1)S(1)}, u32[]{:S(2)}, u32[]{:S(2)}) collective-permute-start(bf16[256,1536]{0,1:T(8,128)(2,1)S(1)} %bitcast.388), channel_id=1, source_target_pairs={{0,16},{16,0},{8,24},{24,8},{1,17},{17,1},{9,25},{25,9},{2,18},{18... | collective-permute-start | bytes 2359304 | tf_op jit(solution)/shard_map/ppermute | solution.py:46
  168.6 28.0 %collective-permute-start.1 = (bf16[256,1536]{0,1:T(8,128)(2,1)S(1)}, bf16[256,1536]{0,1:T(8,128)(2,1)S(1)}, u32[]{:S(2)}, u32[]{:S(2)}) collective-permute-start(bf16[256,1536]{0,1:T(8,128)(2,1)S(1)} %bitcast.389), channel_id=1, source_target_pairs={{0,8},{8,0},{16,24},{24,16},{1,9},{9,1},{17,25},{25,17},{2,10},{10... | collective-permute-start | bytes 2359304 | tf_op jit(solution)/shard_map/ppermute | solution.py:42
  190.3 24.2 %collective-permute-start = (bf16[2,320,1024]{2,1,0:T(8,128)(2,1)S(1)}, bf16[2,320,1024]{2,1,0:T(8,128)(2,1)S(1)}, u32[]{:S(2)}, u32[]{:S(2)}) collective-permute-start(bf16[2,320,1024]{2,1,0:T(8,128)(2,1)S(1)} %copy-done.63), channel_id=1, source_target_pairs={{0,4},{4,0},{1,5},{5,1},{2,6},{6,2},{3,7},{7,3},{8,12},{12,8},{9,1... | collective-permute-start | bytes 3932168 | tf_op jit(solution)/shard_map/ppermute | solution.py:50
  192.8 97.4 %collective-permute-start.22 = (bf16[128,1536]{0,1:T(8,128)(2,1)}, bf16[128,1536]{0,1:T(8,128)(2,1)S(1)}, u32[]{:S(2)}, u32[]{:S(2)}) collective-permute-start(bf16[128,1536]{0,1:T(8,128)(2,1)} %slice.877), channel_id=1, source_target_pairs={{0,8},{8,0},{16,24},{24,16},{1,9},{9,1},{17,25},{25,17},{2,10},{10... | collective-permute-start | bytes 1179656 | tf_op jit(solution)/shard_map/ppermute | solution.py:42
  290.2 31.6 %collective-permute-start.9 = (bf16[592,1024]{1,0:T(8,128)(2,1)}, bf16[592,1024]{1,0:T(8,128)(2,1)}, u32[]{:S(2)}, u32[]{:S(2)}) collective-permute-start(bf16[592,1024]{1,0:T(8,128)(2,1)} %convolution_convert_fusion.5), channel_id=1, source_target_pairs={{0,4},{4,0},{1,5},{5,1},{2,6},{6,2},{3,7},{7,3},{8,12},{12,8},{9,1... | collective-permute-start | bytes 3637256 | tf_op jit(solution)/shard_map/ppermute | solution.py:50
  302.3 60.2 %collective-permute-start.15 = (bf16[256,2048]{0,1:T(8,128)(2,1)}, bf16[256,2048]{0,1:T(8,128)(2,1)}, u32[]{:S(2)}, u32[]{:S(2)}) collective-permute-start(bf16[256,2048]{0,1:T(8,128)(2,1)} %bitcast.41), channel_id=1, source_target_pairs={{0,16},{16,0},{8,24},{24,8},{1,17},{17,1},{9,25},{25,9},{2,18},{18... | collective-permute-start | bytes 3145736 | tf_op jit(solution)/shard_map/ppermute | solution.py:46
  303.9 53.9 %collective-permute-start.14 = (bf16[256,2048]{0,1:T(8,128)(2,1)}, bf16[256,2048]{0,1:T(8,128)(2,1)}, u32[]{:S(2)}, u32[]{:S(2)}) collective-permute-start(bf16[256,2048]{0,1:T(8,128)(2,1)} %bitcast.41), channel_id=1, source_target_pairs={{0,8},{8,0},{16,24},{24,16},{1,9},{9,1},{17,25},{25,17},{2,10},{10... | collective-permute-start | bytes 3145736 | tf_op jit(solution)/shard_map/ppermute | solution.py:42
  310.5 49.1 %collective-permute-start.11 = (bf16[256,2048]{0,1:T(8,128)(2,1)}, bf16[256,2048]{0,1:T(8,128)(2,1)}, u32[]{:S(2)}, u32[]{:S(2)}) collective-permute-start(bf16[256,2048]{0,1:T(8,128)(2,1)} %bitcast.33), channel_id=1, source_target_pairs={{0,16},{16,0},{8,24},{24,8},{1,17},{17,1},{9,25},{25,9},{2,18},{18... | collective-permute-start | bytes 3145736 | tf_op jit(solution)/shard_map/ppermute | solution.py:46
  310.6 43.0 %collective-permute-start.10 = (bf16[256,2048]{0,1:T(8,128)(2,1)}, bf16[256,2048]{0,1:T(8,128)(2,1)}, u32[]{:S(2)}, u32[]{:S(2)}) collective-permute-start(bf16[256,2048]{0,1:T(8,128)(2,1)} %bitcast.33), channel_id=1, source_target_pairs={{0,8},{8,0},{16,24},{24,16},{1,9},{9,1},{17,25},{25,17},{2,10},{10... | collective-permute-start | bytes 3145736 | tf_op jit(solution)/shard_map/ppermute | solution.py:42
  321.8 102.9 %collective-permute-start.33 = (bf16[256,2048]{0,1:T(8,128)(2,1)S(1)}, bf16[256,2048]{0,1:T(8,128)(2,1)S(1)}, u32[]{:S(2)}, u32[]{:S(2)}) collective-permute-start(bf16[256,2048]{0,1:T(8,128)(2,1)S(1)} %bitcast.377), channel_id=1, source_target_pairs={{0,16},{16,0},{8,24},{24,8},{1,17},{17,1},{9,25},{25,9},{2,18},{18... | collective-permute-start | bytes 3145736 | tf_op jit(solution)/shard_map/ppermute | solution.py:46
  353.7 71.9 %collective-permute-start.32 = (bf16[256,2048]{0,1:T(8,128)(2,1)S(1)}, bf16[256,2048]{0,1:T(8,128)(2,1)S(1)}, u32[]{:S(2)}, u32[]{:S(2)}) collective-permute-start(bf16[256,2048]{0,1:T(8,128)(2,1)S(1)} %bitcast.378), channel_id=1, source_target_pairs={{0,8},{8,0},{16,24},{24,16},{1,9},{9,1},{17,25},{25,17},{2,10},{10... | collective-permute-start | bytes 3145736 | tf_op jit(solution)/shard_map/ppermute | solution.py:42
  357.8 26.8 %collective-permute-start.12 = (bf16[128,2048]{0,1:T(8,128)(2,1)S(1)}, bf16[128,2048]{0,1:T(8,128)(2,1)S(1)}, u32[]{:S(2)}, u32[]{:S(2)}) collective-permute-start(bf16[128,2048]{0,1:T(8,128)(2,1)S(1)} %slice.868), channel_id=1, source_target_pairs={{0,16},{16,0},{8,24},{24,8},{1,17},{17,1},{9,25},{25,9},{2,18},{18... | collective-permute-start | bytes 1572872 | tf_op jit(solution)/shard_map/ppermute | solution.py:46
  359.6 68.6 %collective-permute-start.29 = (bf16[256,2048]{0,1:T(8,128)(2,1)S(1)}, bf16[256,2048]{0,1:T(8,128)(2,1)S(1)}, u32[]{:S(2)}, u32[]{:S(2)}) collective-permute-start(bf16[256,2048]{0,1:T(8,128)(2,1)S(1)} %bitcast.374), channel_id=1, source_target_pairs={{0,16},{16,0},{8,24},{24,8},{1,17},{17,1},{9,25},{25,9},{2,18},{18... | collective-permute-start | bytes 3145736 | tf_op jit(solution)/shard_map/ppermute | solution.py:46
  362.5 28.5 %collective-permute-start.13 = (bf16[128,2048]{0,1:T(8,128)(2,1)S(1)}, bf16[128,2048]{0,1:T(8,128)(2,1)S(1)}, u32[]{:S(2)}, u32[]{:S(2)}) collective-permute-start(bf16[128,2048]{0,1:T(8,128)(2,1)S(1)} %slice.869), channel_id=1, source_target_pairs={{0,8},{8,0},{16,24},{24,16},{1,9},{9,1},{17,25},{25,17},{2,10},{10... | collective-permute-start | bytes 1572872 | tf_op jit(solution)/shard_map/ppermute | solution.py:42
  384.6 36.8 %collective-permute-start.17 = (bf16[128,2048]{0,1:T(8,128)(2,1)S(1)}, bf16[128,2048]{0,1:T(8,128)(2,1)S(1)}, u32[]{:S(2)}, u32[]{:S(2)}) collective-permute-start(bf16[128,2048]{0,1:T(8,128)(2,1)S(1)} %slice.872), channel_id=1, source_target_pairs={{0,8},{8,0},{16,24},{24,16},{1,9},{9,1},{17,25},{25,17},{2,10},{10... | collective-permute-start | bytes 1572872 | tf_op jit(solution)/shard_map/ppermute | solution.py:42
  390.9 27.0 %collective-permute-start.16 = (bf16[128,2048]{0,1:T(8,128)(2,1)S(1)}, bf16[128,2048]{0,1:T(8,128)(2,1)S(1)}, u32[]{:S(2)}, u32[]{:S(2)}) collective-permute-start(bf16[128,2048]{0,1:T(8,128)(2,1)S(1)} %slice.871), channel_id=1, source_target_pairs={{0,16},{16,0},{8,24},{24,8},{1,17},{17,1},{9,25},{25,9},{2,18},{18... | collective-permute-start | bytes 1572872 | tf_op jit(solution)/shard_map/ppermute | solution.py:46
  417.9 27.2 %collective-permute-start.28 = (bf16[256,2048]{0,1:T(8,128)(2,1)S(1)}, bf16[256,2048]{0,1:T(8,128)(2,1)S(1)}, u32[]{:S(2)}, u32[]{:S(2)}) collective-permute-start(bf16[256,2048]{0,1:T(8,128)(2,1)S(1)} %bitcast.375), channel_id=1, source_target_pairs={{0,8},{8,0},{16,24},{24,16},{1,9},{9,1},{17,25},{25,17},{2,10},{10... | collective-permute-start | bytes 3145736 | tf_op jit(solution)/shard_map/ppermute | solution.py:42
  425.5 51.7 %collective-permute-start.35 = (bf16[128,2048]{0,1:T(8,128)(2,1)}, bf16[128,2048]{0,1:T(8,128)(2,1)}, u32[]{:S(2)}, u32[]{:S(2)}) collective-permute-start(bf16[128,2048]{0,1:T(8,128)(2,1)} %slice.890), channel_id=1, source_target_pairs={{0,8},{8,0},{16,24},{24,16},{1,9},{9,1},{17,25},{25,17},{2,10},{10... | collective-permute-start | bytes 1572872 | tf_op jit(solution)/shard_map/ppermute | solution.py:42
  426.4 48.9 %collective-permute-start.34 = (bf16[128,2048]{0,1:T(8,128)(2,1)}, bf16[128,2048]{0,1:T(8,128)(2,1)}, u32[]{:S(2)}, u32[]{:S(2)}) collective-permute-start(bf16[128,2048]{0,1:T(8,128)(2,1)} %slice.889), channel_id=1, source_target_pairs={{0,16},{16,0},{8,24},{24,8},{1,17},{17,1},{9,25},{25,9},{2,18},{18... | collective-permute-start | bytes 1572872 | tf_op jit(solution)/shard_map/ppermute | solution.py:46
  429.0 51.4 %collective-permute-start.31 = (bf16[128,2048]{0,1:T(8,128)(2,1)}, bf16[128,2048]{0,1:T(8,128)(2,1)}, u32[]{:S(2)}, u32[]{:S(2)}) collective-permute-start(bf16[128,2048]{0,1:T(8,128)(2,1)} %slice.888), channel_id=1, source_target_pairs={{0,8},{8,0},{16,24},{24,16},{1,9},{9,1},{17,25},{25,17},{2,10},{10... | collective-permute-start | bytes 1572872 | tf_op jit(solution)/shard_map/ppermute | solution.py:42
  446.0 33.2 %collective-permute-start.30 = (bf16[128,2048]{0,1:T(8,128)(2,1)}, bf16[128,2048]{0,1:T(8,128)(2,1)}, u32[]{:S(2)}, u32[]{:S(2)}) collective-permute-start(bf16[128,2048]{0,1:T(8,128)(2,1)} %slice.887), channel_id=1, source_target_pairs={{0,16},{16,0},{8,24},{24,8},{1,17},{17,1},{9,25},{25,9},{2,18},{18... | collective-permute-start | bytes 1572872 | tf_op jit(solution)/shard_map/ppermute | solution.py:46
  500.9 63.1 %collective-permute-start.37 = (bf16[592,1024]{1,0:T(8,128)(2,1)}, bf16[592,1024]{1,0:T(8,128)(2,1)}, u32[]{:S(2)}, u32[]{:S(2)}) collective-permute-start(bf16[592,1024]{1,0:T(8,128)(2,1)} %convolution_convert_fusion.1), channel_id=1, source_target_pairs={{0,4},{4,0},{1,5},{5,1},{2,6},{6,2},{3,7},{7,3},{8,12},{12,8},{9,1... | collective-permute-start | bytes 3637256 | tf_op jit(solution)/shard_map/ppermute | solution.py:50
  502.1 55.8 %collective-permute-start.68 = (bf16[256,2048]{1,0:T(8,128)(2,1)}, bf16[256,2048]{1,0:T(8,128)(2,1)}, u32[]{:S(2)}, u32[]{:S(2)}) collective-permute-start(bf16[256,2048]{1,0:T(8,128)(2,1)} %pad_maximum_fusion.6), channel_id=1, source_target_pairs={{0,16},{16,0},{8,24},{24,8},{1,17},{17,1},{9,25},{25,9},{2,18},{18... | collective-permute-start | bytes 3145736 | tf_op jit(solution)/shard_map/ppermute | solution.py:46
  503.4 26.3 %collective-permute-start.66 = (bf16[256,2048]{1,0:T(8,128)(2,1)}, bf16[256,2048]{1,0:T(8,128)(2,1)}, u32[]{:S(2)}, u32[]{:S(2)}) collective-permute-start(bf16[256,2048]{1,0:T(8,128)(2,1)} %pad_maximum_fusion.5), channel_id=1, source_target_pairs={{0,8},{8,0},{16,24},{24,16},{1,9},{9,1},{17,25},{25,17},{2,10},{10... | collective-permute-start | bytes 3145736 | tf_op jit(solution)/shard_map/ppermute | solution.py:42
  512.8 48.4 %collective-permute-start.78 = (bf16[256,2048]{1,0:T(8,128)(2,1)}, bf16[256,2048]{1,0:T(8,128)(2,1)}, u32[]{:S(2)}, u32[]{:S(2)}) collective-permute-start(bf16[256,2048]{1,0:T(8,128)(2,1)} %pad_maximum_fusion.10), channel_id=1, source_target_pairs={{0,16},{16,0},{8,24},{24,8},{1,17},{17,1},{9,25},{25,9},{2,18},{18... | collective-permute-start | bytes 3145736 | tf_op jit(solution)/shard_map/ppermute | solution.py:46
  515.6 36.3 %collective-permute-start.76 = (bf16[256,2048]{1,0:T(8,128)(2,1)}, bf16[256,2048]{1,0:T(8,128)(2,1)}, u32[]{:S(2)}, u32[]{:S(2)}) collective-permute-start(bf16[256,2048]{1,0:T(8,128)(2,1)} %pad_maximum_fusion.9), channel_id=1, source_target_pairs={{0,8},{8,0},{16,24},{24,16},{1,9},{9,1},{17,25},{25,17},{2,10},{10... | collective-permute-start | bytes 3145736 | tf_op jit(solution)/shard_map/ppermute | solution.py:42
  529.7 37.1 %collective-permute-start.36 = (bf16[592,1024]{1,0:T(8,128)(2,1)}, bf16[592,1024]{1,0:T(8,128)(2,1)S(1)}, u32[]{:S(2)}, u32[]{:S(2)}) collective-permute-start(bf16[592,1024]{1,0:T(8,128)(2,1)} %convolution_convert_fusion.2), channel_id=1, source_target_pairs={{0,4},{4,0},{1,5},{5,1},{2,6},{6,2},{3,7},{7,3},{8,12},{12,8},{9,1... | collective-permute-start | bytes 3637256 | tf_op jit(solution)/shard_map/ppermute | solution.py:50
  551.8 89.8 %collective-permute-start.67 = (bf16[128,2048]{1,0:T(8,128)(2,1)}, bf16[128,2048]{1,0:T(8,128)(2,1)}, u32[]{:S(2)}, u32[]{:S(2)}) collective-permute-start(bf16[128,2048]{1,0:T(8,128)(2,1)} %fusion.48), channel_id=1, source_target_pairs={{0,16},{16,0},{8,24},{24,8},{1,17},{17,1},{9,25},{25,9},{2,18},{18... | collective-permute-start | bytes 1572872 | tf_op jit(solution)/shard_map/ppermute | solution.py:46
  558.0 116.2 %collective-permute-start.77 = (bf16[128,2048]{1,0:T(8,128)(2,1)}, bf16[128,2048]{1,0:T(8,128)(2,1)}, u32[]{:S(2)}, u32[]{:S(2)}) collective-permute-start(bf16[128,2048]{1,0:T(8,128)(2,1)} %fusion.36), channel_id=1, source_target_pairs={{0,16},{16,0},{8,24},{24,8},{1,17},{17,1},{9,25},{25,9},{2,18},{18... | collective-permute-start | bytes 1572872 | tf_op jit(solution)/shard_map/ppermute | solution.py:46
  614.1 26.6 %collective-permute-start.58 = (bf16[256,512]{0,1:T(8,128)(2,1)}, bf16[256,512]{0,1:T(8,128)(2,1)}, u32[]{:S(2)}, u32[]{:S(2)}) collective-permute-start(bf16[256,512]{0,1:T(8,128)(2,1)} %pad_maximum_fusion.22), channel_id=1, source_target_pairs={{0,16},{16,0},{8,24},{24,8},{1,17},{17,1},{9,25},{25,9},{2,18},{18... | collective-permute-start | bytes 786440 | tf_op jit(solution)/shard_map/ppermute | solution.py:46
  636.5 51.5 %collective-permute-start.48 = (bf16[256,1536]{1,0:T(8,128)(2,1)}, bf16[256,1536]{1,0:T(8,128)(2,1)}, u32[]{:S(2)}, u32[]{:S(2)}) collective-permute-start(bf16[256,1536]{1,0:T(8,128)(2,1)} %pad_maximum_fusion.18), channel_id=1, source_target_pairs={{0,16},{16,0},{8,24},{24,8},{1,17},{17,1},{9,25},{25,9},{2,18},{18... | collective-permute-start | bytes 2359304 | tf_op jit(solution)/shard_map/ppermute | solution.py:46
  668.7 298.6 %reduce-scatter.19.cloned.1.call-start = ((), (), s32[]{:S(2)}) async-start(), calls=%async_computation.14 | async-start | bytes 1310720 | tf_op jit(solution)/shard_map/reduce_scatter | solution.py:101
  674.1 293.7 %reduce-scatter.23.cloned.1.call-start = ((), (), s32[]{:S(2)}) async-start(), calls=%async_computation.16 | async-start | bytes 1310720 | tf_op jit(solution)/shard_map/reduce_scatter | solution.py:101
  695.6 274.0 %reduce-scatter.11.cloned.1.call-start = ((), (), s32[]{:S(2)}) async-start(), calls=%async_computation.9 | async-start | bytes 983040 | tf_op jit(solution)/shard_map/reduce_scatter | solution.py:101
  703.4 42.9 %collective-permute-start.49 = (bf16[128,1536]{1,0:T(8,128)(2,1)}, bf16[128,1536]{1,0:T(8,128)(2,1)S(1)}, u32[]{:S(2)}, u32[]{:S(2)}) collective-permute-start(bf16[128,1536]{1,0:T(8,128)(2,1)} %get-tuple-element.109), channel_id=1, source_target_pairs={{0,8},{8,0},{16,24},{24,16},{1,9},{9,1},{17,25},{25,17},{2,10},{10... | collective-permute-start | bytes 1179656 | tf_op jit(solution)/shard_map/ppermute | solution.py:42
  731.8 64.0 %collective-permute-start.39 = (bf16[592,1024]{1,0:T(8,128)(2,1)}, bf16[592,1024]{1,0:T(8,128)(2,1)}, u32[]{:S(2)}, u32[]{:S(2)}) collective-permute-start(bf16[592,1024]{1,0:T(8,128)(2,1)} %convolution_convert_fusion), channel_id=1, source_target_pairs={{0,4},{4,0},{1,5},{5,1},{2,6},{6,2},{3,7},{7,3},{8,12},{12,8},{9,1... | collective-permute-start | bytes 3637256 | tf_op jit(solution)/shard_map/ppermute | solution.py:50
  734.6 55.5 %collective-permute-start.63 = (bf16[256,2048]{1,0:T(8,128)(2,1)}, bf16[256,2048]{1,0:T(8,128)(2,1)}, u32[]{:S(2)}, u32[]{:S(2)}) collective-permute-start(bf16[256,2048]{1,0:T(8,128)(2,1)} %pad_maximum_fusion.4), channel_id=1, source_target_pairs={{0,16},{16,0},{8,24},{24,8},{1,17},{17,1},{9,25},{25,9},{2,18},{18... | collective-permute-start | bytes 3145736 | tf_op jit(solution)/shard_map/ppermute | solution.py:46
  736.1 26.3 %collective-permute-start.61 = (bf16[256,2048]{1,0:T(8,128)(2,1)}, bf16[256,2048]{1,0:T(8,128)(2,1)}, u32[]{:S(2)}, u32[]{:S(2)}) collective-permute-start(bf16[256,2048]{1,0:T(8,128)(2,1)} %pad_maximum_fusion.3), channel_id=1, source_target_pairs={{0,8},{8,0},{16,24},{24,16},{1,9},{9,1},{17,25},{25,17},{2,10},{10... | collective-permute-start | bytes 3145736 | tf_op jit(solution)/shard_map/ppermute | solution.py:42
  743.7 49.1 %collective-permute-start.73 = (bf16[256,2048]{1,0:T(8,128)(2,1)}, bf16[256,2048]{1,0:T(8,128)(2,1)}, u32[]{:S(2)}, u32[]{:S(2)}) collective-permute-start(bf16[256,2048]{1,0:T(8,128)(2,1)} %pad_maximum_fusion.8), channel_id=1, source_target_pairs={{0,16},{16,0},{8,24},{24,8},{1,17},{17,1},{9,25},{25,9},{2,18},{18... | collective-permute-start | bytes 3145736 | tf_op jit(solution)/shard_map/ppermute | solution.py:46
  746.3 37.8 %collective-permute-start.71 = (bf16[256,2048]{1,0:T(8,128)(2,1)}, bf16[256,2048]{1,0:T(8,128)(2,1)}, u32[]{:S(2)}, u32[]{:S(2)}) collective-permute-start(bf16[256,2048]{1,0:T(8,128)(2,1)} %pad_maximum_fusion.7), channel_id=1, source_target_pairs={{0,8},{8,0},{16,24},{24,16},{1,9},{9,1},{17,25},{25,17},{2,10},{10... | collective-permute-start | bytes 3145736 | tf_op jit(solution)/shard_map/ppermute | solution.py:42
  751.1 220.7 %reduce-scatter.13.cloned.1.call-start = ((), (), s32[]{:S(2)}) async-start(), calls=%async_computation.11 | async-start | bytes 327680 | tf_op jit(solution)/shard_map/reduce_scatter | solution.py:101
  766.8 118.7 %collective-permute-start.62 = (bf16[128,2048]{1,0:T(8,128)(2,1)}, bf16[128,2048]{1,0:T(8,128)(2,1)}, u32[]{:S(2)}, u32[]{:S(2)}) collective-permute-start(bf16[128,2048]{1,0:T(8,128)(2,1)} %fusion.54), channel_id=1, source_target_pairs={{0,16},{16,0},{8,24},{24,8},{1,17},{17,1},{9,25},{25,9},{2,18},{18... | collective-permute-start | bytes 1572872 | tf_op jit(solution)/shard_map/ppermute | solution.py:46
  788.5 64.8 %collective-permute-start.72 = (bf16[128,2048]{1,0:T(8,128)(2,1)}, bf16[128,2048]{1,0:T(8,128)(2,1)}, u32[]{:S(2)}, u32[]{:S(2)}) collective-permute-start(bf16[128,2048]{1,0:T(8,128)(2,1)} %fusion.42), channel_id=1, source_target_pairs={{0,16},{16,0},{8,24},{24,8},{1,17},{17,1},{9,25},{25,9},{2,18},{18... | collective-permute-start | bytes 1572872 | tf_op jit(solution)/shard_map/ppermute | solution.py:46
  845.7 31.1 %collective-permute-start.40 = (bf16[592,1024]{1,0:T(8,128)(2,1)}, bf16[592,1024]{1,0:T(8,128)(2,1)}, u32[]{:S(2)}, u32[]{:S(2)}) collective-permute-start(bf16[592,1024]{1,0:T(8,128)(2,1)} %convolution_convert_fusion.6), channel_id=1, source_target_pairs={{0,4},{4,0},{1,5},{5,1},{2,6},{6,2},{3,7},{7,3},{8,12},{12,8},{9,1... | collective-permute-start | bytes 3637256 | tf_op jit(solution)/shard_map/ppermute | solution.py:50
  874.1 141.1 %all-reduce.5.cloned.1.call-start = ((), (), s32[]{:S(2)}) async-start(), calls=%async_computation.10 | async-start | bytes 163840 | tf_op jit(solution)/shard_map/psum | solution.py:316
  880.8 165.8 %reduce-scatter.21.cloned.1.call-start = ((), (), s32[]{:S(2)}) async-start(), calls=%async_computation.15 | async-start | bytes 1310720 | tf_op jit(solution)/shard_map/reduce_scatter | solution.py:101
  882.0 193.3 %reduce-scatter.17.cloned.1.call-start = ((), (), s32[]{:S(2)}) async-start(), calls=%async_computation.13 | async-start | bytes 1310720 | tf_op jit(solution)/shard_map/reduce_scatter | solution.py:101
  890.7 35.2 %collective-permute-start.43 = (bf16[256,1536]{1,0:T(8,128)(2,1)}, bf16[256,1536]{1,0:T(8,128)(2,1)}, u32[]{:S(2)}, u32[]{:S(2)}) collective-permute-start(bf16[256,1536]{1,0:T(8,128)(2,1)} %pad_maximum_fusion.16), channel_id=1, source_target_pairs={{0,16},{16,0},{8,24},{24,8},{1,17},{17,1},{9,25},{25,9},{2,18},{18... | collective-permute-start | bytes 2359304 | tf_op jit(solution)/shard_map/ppermute | solution.py:46
  917.9 182.3 %reduce-scatter.9.cloned.1.call-start = ((), (), s32[]{:S(2)}) async-start(), calls=%async_computation.8 | async-start | bytes 983040 | tf_op jit(solution)/shard_map/reduce_scatter | solution.py:101
  943.2 213.1 %all-gather.29.cloned.1.call-start = ((), (), s32[]{:S(2)}) async-start(), calls=%async_computation.22 | async-start | bytes 3276800 | tf_op jit(solution)/shard_map/all_gather | solution.py:289
  966.5 244.8 %all-gather.27.cloned.1.call-start = ((), (), s32[]{:S(2)}) async-start(), calls=%async_computation.21 | async-start | bytes 3276800 | tf_op jit(solution)/shard_map/all_gather | solution.py:289
  1046.7 53.5 %collective-permute-start.75 = (bf16[256,1,512]{2,0,1:T(8,128)(2,1)}, bf16[256,1,512]{2,0,1:T(8,128)(2,1)S(1)}, u32[]{:S(2)}, u32[]{:S(2)}) collective-permute-start(bf16[256,1,512]{2,0,1:T(8,128)(2,1)} %bitcast.440), channel_id=1, source_target_pairs={{0,4},{4,0},{1,5},{5,1},{2,6},{6,2},{3,7},{7,3},{8,12},{12,8},{9,1... | collective-permute-start | bytes 786440 | tf_op jit(solution)/shard_map/ppermute | solution.py:50
  1075.3 26.2 %collective-permute-start.65 = (bf16[256,1,512]{2,0,1:T(8,128)(2,1)}, bf16[256,1,512]{2,0,1:T(8,128)(2,1)}, u32[]{:S(2)}, u32[]{:S(2)}) collective-permute-start(bf16[256,1,512]{2,0,1:T(8,128)(2,1)} %bitcast.441), channel_id=1, source_target_pairs={{0,4},{4,0},{1,5},{5,1},{2,6},{6,2},{3,7},{7,3},{8,12},{12,8},{9,1... | collective-permute-start | bytes 786440 | tf_op jit(solution)/shard_map/ppermute | solution.py:50
  (165 other events, 1921.1 us)
Sparse Core Ops, SparseCore 0:
  10.2 36.8 all-gather.20
  49.2 35.7 all-gather.18
  87.1 36.1 all-gather.22
  124.8 30.8 all-gather.24
  668.8 16.7 reduce-scatter.14
  687.8 25.4 reduce-scatter.18
  715.6 25.8 reduce-scatter.22
  751.3 20.4 reduce-scatter.10
  874.3 17.6 reduce-scatter.12
  897.4 117.8 all-reduce.4
  1017.6 29.0 reduce-scatter.20
  1049.5 25.7 reduce-scatter.16
  1078.2 21.9 reduce-scatter.8
  1102.2 54.0 all-gather.28
  1157.7 53.5 all-gather.26
where the time goes:
time: 1230 us; the launch traced here: 1220 us
  waiting for transfers between devices  424 us (34%)
  local copies, waits for them, and re-layouts  235 us (19%)
  other arithmetic  203 us (17%)
  matrix products  144 us (12%)
  blocking collectives  117 us (10%)
  starting transfers between devices  77.4 us (6%)
  between operations  20.5 us (2%)
    ppermute x32, waiting for transfers between devices, send_x(): return lax.ppermute(values, 'fsdp', X_PAIRS)  133 us
    all_gather x2, waiting for transfers between devices, give_back(): return lax.all_gather(mine, 'tp', axis=0)[:slots]  100 us
    reduce_scatter x8, waiting for transfers between devices, scatter_matrix(): own = lax.psum_scatter(kept, 'tp', scatter_dimension=0, tiled=False)  79.1 us
    all_gather x4, blocking collectives, gather_matrix(): along = lax.all_gather(half, 'tp', axis=0)  77.4 us
    ppermute x32, waiting for transfers between devices, send_y(): return lax.ppermute(values, 'fsdp', Y_PAIRS)  70.2 us
    unnamed x340, local copies, waits for them, and re-layouts  62.1 us
    dot_general x8, matrix products, mm_tn(): lax.dot_general(left, right, (((0,), (0,)), ((), ())), preferred_element_...  41.5 us
    rev x11, local copies, waits for them, and re-layouts, reorder(): blocks = jnp.where(place % 2 == 1, blocks[..., :, ::-1, :], blocks)  40.8 us
  transfers between devices with their start and end apart: 96, of which 30 were waited for; matrix products, arithmetic and copies ran while one was open for 44% of the time, Pallas kernels for 0%

commit v1 on v0

--- a/solution.py
+++ b/solution.py
@@ -313,7 +313,10 @@
         from_core(jnp.stack([member(0), member(1)], axis=1), 2),
         from_core(member(3)[:, None], 1),
     ] + [reorder(member(k)) * first for k in (2, 4, 5, 6)]
-    summed = lax.psum(jnp.concatenate([a.reshape(-1) for a in joined]), ("fsdp", "ctx", "tp"))
+    summed = jnp.sum(
+        lax.all_gather(jnp.concatenate([a.reshape(-1) for a in joined]), ("fsdp", "ctx", "tp")),
+        axis=0,
+    )
     whole, start = ([], 0)
     for a in joined:
         whole.append(summed[start : start + a.size])

time: 1230 us -> 1160 us (0.943)
  waiting for transfers between devices: 424 us -> 374 us
  other arithmetic: 203 us -> 188 us
    reduce_scatter x8, waiting for transfers between devices: 79.1 us -> 11.9 us  [scatter_matrix(): own = lax.psum_scatter(kept, 'tp', scatter_dimension=0, tiled=False)]
    all_gather x0 -> x1, waiting for transfers between devices: none -> 56.6 us  [shards(): lax.all_gather(jnp.concatenate([a.reshape(-1) for a in joined]), ('fsdp',...]
    psum x1 -> x0, waiting for transfers between devices: 40.2 us -> none  [shards(): lax.psum(jnp.concatenate([a.reshape(-1) for a in joined]), ('fsdp', 'ctx'...]
    ppermute x32, waiting for transfers between devices: 70.2 us -> 86.9 us  [send_y(): return lax.ppermute(values, 'fsdp', Y_PAIRS)]
    ppermute x32, waiting for transfers between devices: 133 us -> 117 us  [send_x(): return lax.ppermute(values, 'fsdp', X_PAIRS)]
    unnamed x340 -> x338, local copies, waits for them, and re-layouts: 62.1 us -> 61.5 us
  transfers between devices with their start and end apart: 96 -> 96, of which waited for: 30 -> 25; matrix products, arithmetic and copies ran while one was open for 44% -> 44% of each run, Pallas kernels for 0% -> 0%
where the time goes in v1:
time: 1160 us; the launch traced here: 1150 us
  waiting for transfers between devices  374 us (32%)
  local copies, waits for them, and re-layouts  230 us (20%)
  other arithmetic  188 us (16%)
  matrix products  138 us (12%)
  blocking collectives  117 us (10%)
  starting transfers between devices  78.7 us (7%)
  between operations  20.7 us (2%)
    ppermute x32, waiting for transfers between devices, send_x(): return lax.ppermute(values, 'fsdp', X_PAIRS)  117 us
    all_gather x2, waiting for transfers between devices, give_back(): return lax.all_gather(mine, 'tp', axis=0)[:slots]  100 us
    ppermute x32, waiting for transfers between devices, send_y(): return lax.ppermute(values, 'fsdp', Y_PAIRS)  86.9 us
    all_gather x4, blocking collectives, gather_matrix(): along = lax.all_gather(half, 'tp', axis=0)  77.4 us
    unnamed x338, local copies, waits for them, and re-layouts  61.5 us
    all_gather x1, waiting for transfers between devices, shards(): lax.all_gather(jnp.concatenate([a.reshape(-1) for a in joined]), ('fsdp',...  56.6 us
    rev x11, local copies, waits for them, and re-layouts, reorder(): blocks = jnp.where(place % 2 == 1, blocks[..., :, ::-1, :], blocks)  40.7 us
    all_gather x1, blocking collectives, shards(): lax.all_gather(packed, ('fsdp', 'tp'), axis=0).reshape(n_fsdp, n_tp, -1)  39.8 us
  transfers between devices with their start and end apart: 96, of which 25 were waited for; matrix products, arithmetic and copies ran while one was open for 44% of the time, Pallas kernels for 0%

profile of v1, /device:TPU:0, one launch (start us, length us, event | category | flops | bytes accessed | tf_op | source)
XLA Modules:
  0.0 1146.7 jit_solution(2988046045456821951)
XLA Ops:
  11.6 16.6 %all-gather.6 = bf16[1024,1,1,128]{0,3,2,1:T(8,128)(2,1)S(1)} all-gather(bf16[256,1,1,128]{0,3,2,1:T(8,128)(2,1)S(1)} %constant_dynamic-slice_fusion.8), channel_id=8, replica_groups=mesh['fsdp'=4,'ctx'=2,'tp'=4] {'tp'}, dimensions={0}, use_global_device_ids=true | all-gather | bytes 327680 | tf_op jit(solution)/shard_map/all_gather | solution.py:91
  31.9 16.8 %all-gather.2 = bf16[1024,1,1,128]{0,3,2,1:T(8,128)(2,1)S(1)} all-gather(bf16[256,1,1,128]{0,3,2,1:T(8,128)(2,1)S(1)} %constant_dynamic-slice_fusion.12), channel_id=4, replica_groups=mesh['fsdp'=4,'ctx'=2,'tp'=4] {'tp'}, dimensions={0}, use_global_device_ids=true | all-gather | bytes 327680 | tf_op jit(solution)/shard_map/all_gather | solution.py:91
  50.7 24.3 %all-gather.5 = bf16[1024,3,1,128]{0,3,2,1:T(8,128)(2,1)S(1)} all-gather(bf16[256,3,1,128]{0,3,2,1:T(8,128)(2,1)S(1)} %constant_dynamic-slice_fusion.9), channel_id=7, replica_groups=mesh['fsdp'=4,'ctx'=2,'tp'=4] {'tp'}, dimensions={0}, use_global_device_ids=true | all-gather | bytes 983040 | tf_op jit(solution)/shard_map/all_gather | solution.py:91
  80.7 39.8 %all-gather.12 = bf16[16,1,2816]{2,1,0:T(2,128)(2,1)S(1)} all-gather(bf16[1,1,2816]{2,1,0:T(2,128)(2,1)S(1)} %reshape.1169), channel_id=2, replica_groups=mesh['fsdp'=4,'ctx'=2,'tp'=4] {'fsdp','tp'}, dimensions={0}, use_global_device_ids=true | all-gather | bytes 95744 | tf_op jit(solution)/shard_map/all_gather | solution.py:236
  126.1 19.7 %all-gather.1 = bf16[1024,3,1,128]{0,3,2,1:T(8,128)(2,1)S(1)} all-gather(bf16[256,3,1,128]{0,3,2,1:T(8,128)(2,1)S(1)} %constant_dynamic-slice_fusion.13), channel_id=3, replica_groups=mesh['fsdp'=4,'ctx'=2,'tp'=4] {'tp'}, dimensions={0}, use_global_device_ids=true | all-gather | bytes 983040 | tf_op jit(solution)/shard_map/all_gather | solution.py:91
  173.0 6.3 collective-permute-done.25
  205.3 6.9 collective-permute-done.3
  215.4 9.2 dynamic_update_slice.3
  226.3 5.7 reshape.1095
  232.0 19.3 %rev.66 = bf16[2,592,2,2,256]{4,3,2,1,0:T(2,128)(2,1)} reverse(bf16[2,592,2,2,256]{4,3,2,1,0:T(2,128)(2,1)S(1)} %reshape.1095), dimensions={3} | reverse | bytes 4849664 | tf_op jit(solution)/shard_map/rev | solution.py:36
  256.3 5.0 fusion.120
  261.3 3.7 squeeze.95
  265.5 4.5 fusion.106
  276.9 3.6 fusion.134
  290.1 4.3 squeeze.100
  295.0 3.6 convert_reduce_fusion.2
  303.1 3.4 collective-permute-start.14
  325.4 27.4 %collective-permute-done.10 = bf16[256,2048]{0,1:T(8,128)(2,1)} collective-permute-done((bf16[256,2048]{0,1:T(8,128)(2,1)}, bf16[256,2048]{0,1:T(8,128)(2,1)}, u32[]{:S(2)}, u32[]{:S(2)}) %collective-permute-start.10) | collective-permute-done | bytes 1048608 | tf_op jit(solution)/shard_map/ppermute | solution.py:42
  366.9 16.8 %collective-permute-done.12 = bf16[128,2048]{0,1:T(8,128)(2,1)S(1)} collective-permute-done((bf16[128,2048]{0,1:T(8,128)(2,1)S(1)}, bf16[128,2048]{0,1:T(8,128)(2,1)S(1)}, u32[]{:S(2)}, u32[]{:S(2)}) %collective-permute-start.12) | collective-permute-done | bytes 524320 | tf_op jit(solution)/shard_map/ppermute | solution.py:46
  383.7 3.2 collective-permute-start.17
  390.4 5.3 multiply_convert_fusion.3
  395.6 21.4 %collective-permute-done.16 = bf16[128,2048]{0,1:T(8,128)(2,1)S(1)} collective-permute-done((bf16[128,2048]{0,1:T(8,128)(2,1)S(1)}, bf16[128,2048]{0,1:T(8,128)(2,1)S(1)}, u32[]{:S(2)}, u32[]{:S(2)}) %collective-permute-start.16) | collective-permute-done | bytes 524320 | tf_op jit(solution)/shard_map/ppermute | solution.py:46
  417.1 3.3 collective-permute-start.28
  430.2 14.2 %collective-permute-done.28 = bf16[256,2048]{0,1:T(8,128)(2,1)S(1)} collective-permute-done((bf16[256,2048]{0,1:T(8,128)(2,1)S(1)}, bf16[256,2048]{0,1:T(8,128)(2,1)S(1)}, u32[]{:S(2)}, u32[]{:S(2)}) %collective-permute-start.28) | collective-permute-done | bytes 1048608 | tf_op jit(solution)/shard_map/ppermute | solution.py:42
  460.8 3.6 fusion.135
  484.0 6.2 convert_reduce_fusion
  492.9 3.7 fusion.140
  500.8 3.5 fusion.142
  512.3 12.6 %collective-permute-done.66 = bf16[256,2048]{1,0:T(8,128)(2,1)} collective-permute-done((bf16[256,2048]{1,0:T(8,128)(2,1)S(1)}, bf16[256,2048]{1,0:T(8,128)(2,1)}, u32[]{:S(2)}, u32[]{:S(2)}) %collective-permute-start.66) | collective-permute-done | bytes 1048608 | tf_op jit(solution)/shard_map/ppermute | solution.py:42
  527.4 19.8 %collective-permute-done.76 = bf16[256,2048]{1,0:T(8,128)(2,1)S(1)} collective-permute-done((bf16[256,2048]{1,0:T(8,128)(2,1)S(1)}, bf16[256,2048]{1,0:T(8,128)(2,1)S(1)}, u32[]{:S(2)}, u32[]{:S(2)}) %collective-permute-start.76) | collective-permute-done | bytes 1048608 | tf_op jit(solution)/shard_map/ppermute | solution.py:42
  566.6 7.4 convert_reduce_fusion.6
  574.0 8.5 multiply_reduce_fusion.1
  582.6 6.6 multiply_convert_fusion.1
  596.1 6.5 fusion.136
  602.5 4.1 reshape.1124
  606.7 12.4 %rev.76 = bf16[592,2,2,256]{3,2,1,0:T(2,128)(2,1)} reverse(bf16[592,2,2,256]{3,2,1,0:T(2,128)(2,1)} %reshape.1124), dimensions={2} | reverse | bytes 2424832 | tf_op jit(solution)/shard_map/rev | solution.py:36
  619.1 3.7 broadcast_select_fusion.3
  627.9 4.2 collective-permute-done.56
  638.3 12.0 %collective-permute-done.57 = bf16[128,512]{0,1:T(8,128)(2,1)S(1)} collective-permute-done((bf16[128,512]{0,1:T(8,128)(2,1)S(1)}, bf16[128,512]{0,1:T(8,128)(2,1)S(1)}, u32[]{:S(2)}, u32[]{:S(2)}) %collective-permute-start.57) | collective-permute-done | bytes 131104 | tf_op jit(solution)/shard_map/ppermute | solution.py:46
  667.0 3.7 fusion.38
  674.6 4.0 reshape.1125
  708.0 6.7 convert_reduce_fusion.1
  714.7 3.7 convolution_convert_fusion
  718.5 6.0 fusion.141
  730.2 5.6 fusion.143
  742.6 12.3 %collective-permute-done.61 = bf16[256,2048]{1,0:T(8,128)(2,1)} collective-permute-done((bf16[256,2048]{1,0:T(8,128)(2,1)}, bf16[256,2048]{1,0:T(8,128)(2,1)}, u32[]{:S(2)}, u32[]{:S(2)}) %collective-permute-start.61) | collective-permute-done | bytes 1048608 | tf_op jit(solution)/shard_map/ppermute | solution.py:42
  759.5 17.1 %collective-permute-done.71 = bf16[256,2048]{1,0:T(8,128)(2,1)} collective-permute-done((bf16[256,2048]{1,0:T(8,128)(2,1)}, bf16[256,2048]{1,0:T(8,128)(2,1)}, u32[]{:S(2)}, u32[]{:S(2)}) %collective-permute-start.71) | collective-permute-done | bytes 1048608 | tf_op jit(solution)/shard_map/ppermute | solution.py:42
  797.9 6.6 convert_reduce_fusion.7
  804.5 9.2 multiply_reduce_fusion
  813.8 6.1 multiply_convert_fusion
  827.0 5.6 fusion.137
  836.9 3.2 fusion.44
  840.5 14.2 %collective-permute-done.52 = bf16[128,512]{0,1:T(8,128)(2,1)S(1)} collective-permute-done((bf16[128,512]{0,1:T(8,128)(2,1)S(1)}, bf16[128,512]{0,1:T(8,128)(2,1)S(1)}, u32[]{:S(2)}, u32[]{:S(2)}) %collective-permute-start.52) | collective-permute-done | bytes 131104 | tf_op jit(solution)/shard_map/ppermute | solution.py:46
  873.4 3.9 fusion.56
  877.6 3.1 convolution_convert_fusion.6
  895.0 3.6 collective-permute-done.42
  906.9 4.1 fusion.113
  920.4 3.4 reshape.1134
  923.8 8.2 rev.78
  935.6 3.2 reshape.1135
  951.3 11.8 %reduce-scatter.9.cloned.1.call-done = bf16[1,256,3,128]{3,1,2,0:T(8,128)(2,1)} async-done(((bf16[4,256,3,128]{3,1,2,0:T(8,128)(2,1)}), bf16[1,256,3,128]{3,1,2,0:T(8,128)(2,1)}) %reduce-scatter.9.cloned.1.call-update) | async-done | bytes 196624 | tf_op jit(solution)/shard_map/reduce_scatter | solution.py:101
  971.2 48.2 %all-gather.31.cloned.1.call-done = bf16[1280,1024]{1,0:T(8,128)(2,1)} async-done(((bf16[320,1024]{1,0:T(8,128)(2,1)}), bf16[1280,1024]{1,0:T(8,128)(2,1)}) %all-gather.31.cloned.1.call-update) | async-done | bytes 2621456 | tf_op jit(solution)/shard_map/all_gather | solution.py:289
  1022.3 52.1 %all-gather.29.cloned.1.call-done = bf16[1280,1024]{1,0:T(8,128)(2,1)} async-done(((bf16[320,1024]{1,0:T(8,128)(2,1)}), bf16[1280,1024]{1,0:T(8,128)(2,1)}) %all-gather.29.cloned.1.call-update) | async-done | bytes 2621456 | tf_op jit(solution)/shard_map/all_gather | solution.py:289
  1077.4 56.6 %all-gather.33.cloned.1.call-done = f32[655360]{0:T(1024)} async-done(((f32[20480]{0:T(1024)}), f32[655360]{0:T(1024)}) %all-gather.33.cloned.1.call-update) | async-done | bytes 2621456 | tf_op jit(solution)/shard_map/all_gather | solution.py:317
  (865 shorter events, 424.3 us)
Async XLA Ops:
  7.2 291.4 %all-gather.23.cloned.1.call-start = ((), (), s32[]{:S(2)}) async-start(), calls=%async_computation.17 | async-start | bytes 1310720 | tf_op jit(solution)/shard_map/all_gather | solution.py:91
  9.4 297.1 %all-gather.21.cloned.1.call-start = ((), (), s32[]{:S(2)}) async-start(), calls=%async_computation.16 | async-start | bytes 1310720 | tf_op jit(solution)/shard_map/all_gather | solution.py:91
  10.5 299.1 %all-gather.25.cloned.1.call-start = ((), (), s32[]{:S(2)}) async-start(), calls=%async_computation.18 | async-start | bytes 1310720 | tf_op jit(solution)/shard_map/all_gather | solution.py:91
  11.5 301.9 %all-gather.27.cloned.1.call-start = ((), (), s32[]{:S(2)}) async-start(), calls=%async_computation.19 | async-start | bytes 1310720 | tf_op jit(solution)/shard_map/all_gather | solution.py:91
  28.6 123.3 %collective-permute-start.24 = (bf16[256,512]{0,1:T(8,128)(2,1)S(1)}, bf16[256,512]{0,1:T(8,128)(2,1)}, u32[]{:S(2)}, u32[]{:S(2)}) collective-permute-start(bf16[256,512]{0,1:T(8,128)(2,1)S(1)} %bitcast.413), channel_id=1, source_target_pairs={{0,16},{16,0},{8,24},{24,8},{1,17},{17,1},{9,25},{25,9},{2,18},{18... | collective-permute-start | bytes 786440 | tf_op jit(solution)/shard_map/ppermute | solution.py:46
  30.3 131.6 %collective-permute-start.23 = (bf16[256,512]{0,1:T(8,128)(2,1)S(1)}, bf16[256,512]{0,1:T(8,128)(2,1)}, u32[]{:S(2)}, u32[]{:S(2)}) collective-permute-start(bf16[256,512]{0,1:T(8,128)(2,1)S(1)} %bitcast.414), channel_id=1, source_target_pairs={{0,8},{8,0},{16,24},{24,16},{1,9},{9,1},{17,25},{25,17},{2,10},{10... | collective-permute-start | bytes 786440 | tf_op jit(solution)/shard_map/ppermute | solution.py:42
  49.0 115.9 %collective-permute-start.6 = (bf16[256,512]{0,1:T(8,128)(2,1)S(1)}, bf16[256,512]{0,1:T(8,128)(2,1)}, u32[]{:S(2)}, u32[]{:S(2)}) collective-permute-start(bf16[256,512]{0,1:T(8,128)(2,1)S(1)} %bitcast.410), channel_id=1, source_target_pairs={{0,16},{16,0},{8,24},{24,8},{1,17},{17,1},{9,25},{25,9},{2,18},{18... | collective-permute-start | bytes 786440 | tf_op jit(solution)/shard_map/ppermute | solution.py:46
  49.6 118.3 %collective-permute-start.5 = (bf16[256,512]{0,1:T(8,128)(2,1)S(1)}, bf16[256,512]{0,1:T(8,128)(2,1)}, u32[]{:S(2)}, u32[]{:S(2)}) collective-permute-start(bf16[256,512]{0,1:T(8,128)(2,1)S(1)} %bitcast.411), channel_id=1, source_target_pairs={{0,8},{8,0},{16,24},{24,16},{1,9},{9,1},{17,25},{25,17},{2,10},{10... | collective-permute-start | bytes 786440 | tf_op jit(solution)/shard_map/ppermute | solution.py:42
  75.6 114.7 %collective-permute-start.20 = (bf16[256,1536]{0,1:T(8,128)(2,1)S(1)}, bf16[256,1536]{0,1:T(8,128)(2,1)}, u32[]{:S(2)}, u32[]{:S(2)}) collective-permute-start(bf16[256,1536]{0,1:T(8,128)(2,1)S(1)} %bitcast.384), channel_id=1, source_target_pairs={{0,16},{16,0},{8,24},{24,8},{1,17},{17,1},{9,25},{25,9},{2,18},{18... | collective-permute-start | bytes 2359304 | tf_op jit(solution)/shard_map/ppermute | solution.py:46
  77.8 865.1 %reduce-scatter.15.cloned.1.call-start = ((), (), s32[]{:S(2)}) async-start(), calls=%async_computation.11 | async-start | bytes 327680 | tf_op jit(solution)/shard_map/reduce_scatter | solution.py:101
  161.9 30.5 %collective-permute-start.19 = (bf16[256,1536]{0,1:T(8,128)(2,1)S(1)}, bf16[256,1536]{0,1:T(8,128)(2,1)S(1)}, u32[]{:S(2)}, u32[]{:S(2)}) collective-permute-start(bf16[256,1536]{0,1:T(8,128)(2,1)S(1)} %bitcast.386), channel_id=1, source_target_pairs={{0,8},{8,0},{16,24},{24,16},{1,9},{9,1},{17,25},{25,17},{2,10},{10... | collective-permute-start | bytes 2359304 | tf_op jit(solution)/shard_map/ppermute | solution.py:42
  164.9 29.1 %collective-permute-start.2 = (bf16[256,1536]{0,1:T(8,128)(2,1)S(1)}, bf16[256,1536]{0,1:T(8,128)(2,1)S(1)}, u32[]{:S(2)}, u32[]{:S(2)}) collective-permute-start(bf16[256,1536]{0,1:T(8,128)(2,1)S(1)} %bitcast.388), channel_id=1, source_target_pairs={{0,16},{16,0},{8,24},{24,8},{1,17},{17,1},{9,25},{25,9},{2,18},{18... | collective-permute-start | bytes 2359304 | tf_op jit(solution)/shard_map/ppermute | solution.py:46
  168.0 28.0 %collective-permute-start.1 = (bf16[256,1536]{0,1:T(8,128)(2,1)S(1)}, bf16[256,1536]{0,1:T(8,128)(2,1)S(1)}, u32[]{:S(2)}, u32[]{:S(2)}) collective-permute-start(bf16[256,1536]{0,1:T(8,128)(2,1)S(1)} %bitcast.389), channel_id=1, source_target_pairs={{0,8},{8,0},{16,24},{24,16},{1,9},{9,1},{17,25},{25,17},{2,10},{10... | collective-permute-start | bytes 2359304 | tf_op jit(solution)/shard_map/ppermute | solution.py:42
  189.7 24.2 %collective-permute-start = (bf16[2,320,1024]{2,1,0:T(8,128)(2,1)S(1)}, bf16[2,320,1024]{2,1,0:T(8,128)(2,1)S(1)}, u32[]{:S(2)}, u32[]{:S(2)}) collective-permute-start(bf16[2,320,1024]{2,1,0:T(8,128)(2,1)S(1)} %copy-done.60), channel_id=1, source_target_pairs={{0,4},{4,0},{1,5},{5,1},{2,6},{6,2},{3,7},{7,3},{8,12},{12,8},{9,1... | collective-permute-start | bytes 3932168 | tf_op jit(solution)/shard_map/ppermute | solution.py:50
  192.1 97.2 %collective-permute-start.22 = (bf16[128,1536]{0,1:T(8,128)(2,1)}, bf16[128,1536]{0,1:T(8,128)(2,1)S(1)}, u32[]{:S(2)}, u32[]{:S(2)}) collective-permute-start(bf16[128,1536]{0,1:T(8,128)(2,1)} %slice.877), channel_id=1, source_target_pairs={{0,8},{8,0},{16,24},{24,16},{1,9},{9,1},{17,25},{25,17},{2,10},{10... | collective-permute-start | bytes 1179656 | tf_op jit(solution)/shard_map/ppermute | solution.py:42
  289.3 31.4 %collective-permute-start.9 = (bf16[592,1024]{1,0:T(8,128)(2,1)}, bf16[592,1024]{1,0:T(8,128)(2,1)}, u32[]{:S(2)}, u32[]{:S(2)}) collective-permute-start(bf16[592,1024]{1,0:T(8,128)(2,1)} %convolution_convert_fusion.5), channel_id=1, source_target_pairs={{0,4},{4,0},{1,5},{5,1},{2,6},{6,2},{3,7},{7,3},{8,12},{12,8},{9,1... | collective-permute-start | bytes 3637256 | tf_op jit(solution)/shard_map/ppermute | solution.py:50
  301.4 60.2 %collective-permute-start.15 = (bf16[256,2048]{0,1:T(8,128)(2,1)}, bf16[256,2048]{0,1:T(8,128)(2,1)}, u32[]{:S(2)}, u32[]{:S(2)}) collective-permute-start(bf16[256,2048]{0,1:T(8,128)(2,1)} %bitcast.41), channel_id=1, source_target_pairs={{0,16},{16,0},{8,24},{24,8},{1,17},{17,1},{9,25},{25,9},{2,18},{18... | collective-permute-start | bytes 3145736 | tf_op jit(solution)/shard_map/ppermute | solution.py:46
  303.1 53.9 %collective-permute-start.14 = (bf16[256,2048]{0,1:T(8,128)(2,1)}, bf16[256,2048]{0,1:T(8,128)(2,1)}, u32[]{:S(2)}, u32[]{:S(2)}) collective-permute-start(bf16[256,2048]{0,1:T(8,128)(2,1)} %bitcast.41), channel_id=1, source_target_pairs={{0,8},{8,0},{16,24},{24,16},{1,9},{9,1},{17,25},{25,17},{2,10},{10... | collective-permute-start | bytes 3145736 | tf_op jit(solution)/shard_map/ppermute | solution.py:42
  309.5 49.3 %collective-permute-start.11 = (bf16[256,2048]{0,1:T(8,128)(2,1)}, bf16[256,2048]{0,1:T(8,128)(2,1)}, u32[]{:S(2)}, u32[]{:S(2)}) collective-permute-start(bf16[256,2048]{0,1:T(8,128)(2,1)} %bitcast.33), channel_id=1, source_target_pairs={{0,16},{16,0},{8,24},{24,8},{1,17},{17,1},{9,25},{25,9},{2,18},{18... | collective-permute-start | bytes 3145736 | tf_op jit(solution)/shard_map/ppermute | solution.py:46
  309.6 43.3 %collective-permute-start.10 = (bf16[256,2048]{0,1:T(8,128)(2,1)}, bf16[256,2048]{0,1:T(8,128)(2,1)}, u32[]{:S(2)}, u32[]{:S(2)}) collective-permute-start(bf16[256,2048]{0,1:T(8,128)(2,1)} %bitcast.33), channel_id=1, source_target_pairs={{0,8},{8,0},{16,24},{24,16},{1,9},{9,1},{17,25},{25,17},{2,10},{10... | collective-permute-start | bytes 3145736 | tf_op jit(solution)/shard_map/ppermute | solution.py:42
  320.8 103.1 %collective-permute-start.33 = (bf16[256,2048]{0,1:T(8,128)(2,1)S(1)}, bf16[256,2048]{0,1:T(8,128)(2,1)S(1)}, u32[]{:S(2)}, u32[]{:S(2)}) collective-permute-start(bf16[256,2048]{0,1:T(8,128)(2,1)S(1)} %bitcast.377), channel_id=1, source_target_pairs={{0,16},{16,0},{8,24},{24,8},{1,17},{17,1},{9,25},{25,9},{2,18},{18... | collective-permute-start | bytes 3145736 | tf_op jit(solution)/shard_map/ppermute | solution.py:46
  352.8 71.9 %collective-permute-start.32 = (bf16[256,2048]{0,1:T(8,128)(2,1)S(1)}, bf16[256,2048]{0,1:T(8,128)(2,1)S(1)}, u32[]{:S(2)}, u32[]{:S(2)}) collective-permute-start(bf16[256,2048]{0,1:T(8,128)(2,1)S(1)} %bitcast.378), channel_id=1, source_target_pairs={{0,8},{8,0},{16,24},{24,16},{1,9},{9,1},{17,25},{25,17},{2,10},{10... | collective-permute-start | bytes 3145736 | tf_op jit(solution)/shard_map/ppermute | solution.py:42
  357.0 26.8 %collective-permute-start.12 = (bf16[128,2048]{0,1:T(8,128)(2,1)S(1)}, bf16[128,2048]{0,1:T(8,128)(2,1)S(1)}, u32[]{:S(2)}, u32[]{:S(2)}) collective-permute-start(bf16[128,2048]{0,1:T(8,128)(2,1)S(1)} %slice.868), channel_id=1, source_target_pairs={{0,16},{16,0},{8,24},{24,8},{1,17},{17,1},{9,25},{25,9},{2,18},{18... | collective-permute-start | bytes 1572872 | tf_op jit(solution)/shard_map/ppermute | solution.py:46
  358.8 68.5 %collective-permute-start.29 = (bf16[256,2048]{0,1:T(8,128)(2,1)S(1)}, bf16[256,2048]{0,1:T(8,128)(2,1)S(1)}, u32[]{:S(2)}, u32[]{:S(2)}) collective-permute-start(bf16[256,2048]{0,1:T(8,128)(2,1)S(1)} %bitcast.374), channel_id=1, source_target_pairs={{0,16},{16,0},{8,24},{24,8},{1,17},{17,1},{9,25},{25,9},{2,18},{18... | collective-permute-start | bytes 3145736 | tf_op jit(solution)/shard_map/ppermute | solution.py:46
  361.6 28.5 %collective-permute-start.13 = (bf16[128,2048]{0,1:T(8,128)(2,1)S(1)}, bf16[128,2048]{0,1:T(8,128)(2,1)S(1)}, u32[]{:S(2)}, u32[]{:S(2)}) collective-permute-start(bf16[128,2048]{0,1:T(8,128)(2,1)S(1)} %slice.869), channel_id=1, source_target_pairs={{0,8},{8,0},{16,24},{24,16},{1,9},{9,1},{17,25},{25,17},{2,10},{10... | collective-permute-start | bytes 1572872 | tf_op jit(solution)/shard_map/ppermute | solution.py:42
  383.7 36.8 %collective-permute-start.17 = (bf16[128,2048]{0,1:T(8,128)(2,1)S(1)}, bf16[128,2048]{0,1:T(8,128)(2,1)S(1)}, u32[]{:S(2)}, u32[]{:S(2)}) collective-permute-start(bf16[128,2048]{0,1:T(8,128)(2,1)S(1)} %slice.872), channel_id=1, source_target_pairs={{0,8},{8,0},{16,24},{24,16},{1,9},{9,1},{17,25},{25,17},{2,10},{10... | collective-permute-start | bytes 1572872 | tf_op jit(solution)/shard_map/ppermute | solution.py:42
  390.1 26.9 %collective-permute-start.16 = (bf16[128,2048]{0,1:T(8,128)(2,1)S(1)}, bf16[128,2048]{0,1:T(8,128)(2,1)S(1)}, u32[]{:S(2)}, u32[]{:S(2)}) collective-permute-start(bf16[128,2048]{0,1:T(8,128)(2,1)S(1)} %slice.871), channel_id=1, source_target_pairs={{0,16},{16,0},{8,24},{24,8},{1,17},{17,1},{9,25},{25,9},{2,18},{18... | collective-permute-start | bytes 1572872 | tf_op jit(solution)/shard_map/ppermute | solution.py:46
  417.1 27.3 %collective-permute-start.28 = (bf16[256,2048]{0,1:T(8,128)(2,1)S(1)}, bf16[256,2048]{0,1:T(8,128)(2,1)S(1)}, u32[]{:S(2)}, u32[]{:S(2)}) collective-permute-start(bf16[256,2048]{0,1:T(8,128)(2,1)S(1)} %bitcast.375), channel_id=1, source_target_pairs={{0,8},{8,0},{16,24},{24,16},{1,9},{9,1},{17,25},{25,17},{2,10},{10... | collective-permute-start | bytes 3145736 | tf_op jit(solution)/shard_map/ppermute | solution.py:42
  424.7 51.2 %collective-permute-start.35 = (bf16[128,2048]{0,1:T(8,128)(2,1)}, bf16[128,2048]{0,1:T(8,128)(2,1)}, u32[]{:S(2)}, u32[]{:S(2)}) collective-permute-start(bf16[128,2048]{0,1:T(8,128)(2,1)} %slice.890), channel_id=1, source_target_pairs={{0,8},{8,0},{16,24},{24,16},{1,9},{9,1},{17,25},{25,17},{2,10},{10... | collective-permute-start | bytes 1572872 | tf_op jit(solution)/shard_map/ppermute | solution.py:42
  425.5 49.1 %collective-permute-start.34 = (bf16[128,2048]{0,1:T(8,128)(2,1)}, bf16[128,2048]{0,1:T(8,128)(2,1)}, u32[]{:S(2)}, u32[]{:S(2)}) collective-permute-start(bf16[128,2048]{0,1:T(8,128)(2,1)} %slice.889), channel_id=1, source_target_pairs={{0,16},{16,0},{8,24},{24,8},{1,17},{17,1},{9,25},{25,9},{2,18},{18... | collective-permute-start | bytes 1572872 | tf_op jit(solution)/shard_map/ppermute | solution.py:46
  428.2 50.7 %collective-permute-start.31 = (bf16[128,2048]{0,1:T(8,128)(2,1)}, bf16[128,2048]{0,1:T(8,128)(2,1)}, u32[]{:S(2)}, u32[]{:S(2)}) collective-permute-start(bf16[128,2048]{0,1:T(8,128)(2,1)} %slice.888), channel_id=1, source_target_pairs={{0,8},{8,0},{16,24},{24,16},{1,9},{9,1},{17,25},{25,17},{2,10},{10... | collective-permute-start | bytes 1572872 | tf_op jit(solution)/shard_map/ppermute | solution.py:42
  445.2 32.0 %collective-permute-start.30 = (bf16[128,2048]{0,1:T(8,128)(2,1)}, bf16[128,2048]{0,1:T(8,128)(2,1)}, u32[]{:S(2)}, u32[]{:S(2)}) collective-permute-start(bf16[128,2048]{0,1:T(8,128)(2,1)} %slice.887), channel_id=1, source_target_pairs={{0,16},{16,0},{8,24},{24,8},{1,17},{17,1},{9,25},{25,9},{2,18},{18... | collective-permute-start | bytes 1572872 | tf_op jit(solution)/shard_map/ppermute | solution.py:46
  496.7 58.4 %collective-permute-start.37 = (bf16[592,1024]{1,0:T(8,128)(2,1)S(1)}, bf16[592,1024]{1,0:T(8,128)(2,1)S(1)}, u32[]{:S(2)}, u32[]{:S(2)}) collective-permute-start(bf16[592,1024]{1,0:T(8,128)(2,1)S(1)} %convolution_convert_fusion.1), channel_id=1, source_target_pairs={{0,4},{4,0},{1,5},{5,1},{2,6},{6,2},{3,7},{7,3},{8,12},{12,8},{9,1... | collective-permute-start | bytes 3637256 | tf_op jit(solution)/shard_map/ppermute | solution.py:50
  498.3 52.1 %collective-permute-start.68 = (bf16[256,2048]{1,0:T(8,128)(2,1)}, bf16[256,2048]{1,0:T(8,128)(2,1)}, u32[]{:S(2)}, u32[]{:S(2)}) collective-permute-start(bf16[256,2048]{1,0:T(8,128)(2,1)} %pad_maximum_fusion.6), channel_id=1, source_target_pairs={{0,16},{16,0},{8,24},{24,8},{1,17},{17,1},{9,25},{25,9},{2,18},{18... | collective-permute-start | bytes 3145736 | tf_op jit(solution)/shard_map/ppermute | solution.py:46
  498.7 26.2 %collective-permute-start.66 = (bf16[256,2048]{1,0:T(8,128)(2,1)S(1)}, bf16[256,2048]{1,0:T(8,128)(2,1)}, u32[]{:S(2)}, u32[]{:S(2)}) collective-permute-start(bf16[256,2048]{1,0:T(8,128)(2,1)S(1)} %pad_maximum_fusion.5), channel_id=1, source_target_pairs={{0,8},{8,0},{16,24},{24,16},{1,9},{9,1},{17,25},{25,17},{2,10},{10... | collective-permute-start | bytes 3145736 | tf_op jit(solution)/shard_map/ppermute | solution.py:42
  504.6 48.9 %collective-permute-start.78 = (bf16[256,2048]{1,0:T(8,128)(2,1)S(1)}, bf16[256,2048]{1,0:T(8,128)(2,1)S(1)}, u32[]{:S(2)}, u32[]{:S(2)}) collective-permute-start(bf16[256,2048]{1,0:T(8,128)(2,1)S(1)} %pad_maximum_fusion.10), channel_id=1, source_target_pairs={{0,16},{16,0},{8,24},{24,8},{1,17},{17,1},{9,25},{25,9},{2,18},{18... | collective-permute-start | bytes 3145736 | tf_op jit(solution)/shard_map/ppermute | solution.py:46
  506.5 40.6 %collective-permute-start.76 = (bf16[256,2048]{1,0:T(8,128)(2,1)S(1)}, bf16[256,2048]{1,0:T(8,128)(2,1)S(1)}, u32[]{:S(2)}, u32[]{:S(2)}) collective-permute-start(bf16[256,2048]{1,0:T(8,128)(2,1)S(1)} %pad_maximum_fusion.9), channel_id=1, source_target_pairs={{0,8},{8,0},{16,24},{24,16},{1,9},{9,1},{17,25},{25,17},{2,10},{10... | collective-permute-start | bytes 3145736 | tf_op jit(solution)/shard_map/ppermute | solution.py:42
  524.9 31.7 %collective-permute-start.36 = (bf16[592,1024]{1,0:T(8,128)(2,1)S(1)}, bf16[592,1024]{1,0:T(8,128)(2,1)S(1)}, u32[]{:S(2)}, u32[]{:S(2)}) collective-permute-start(bf16[592,1024]{1,0:T(8,128)(2,1)S(1)} %convolution_convert_fusion.2), channel_id=1, source_target_pairs={{0,4},{4,0},{1,5},{5,1},{2,6},{6,2},{3,7},{7,3},{8,12},{12,8},{9,1... | collective-permute-start | bytes 3637256 | tf_op jit(solution)/shard_map/ppermute | solution.py:50
  547.2 86.5 %collective-permute-start.67 = (bf16[128,2048]{1,0:T(8,128)(2,1)}, bf16[128,2048]{1,0:T(8,128)(2,1)}, u32[]{:S(2)}, u32[]{:S(2)}) collective-permute-start(bf16[128,2048]{1,0:T(8,128)(2,1)} %fusion.48), channel_id=1, source_target_pairs={{0,16},{16,0},{8,24},{24,8},{1,17},{17,1},{9,25},{25,9},{2,18},{18... | collective-permute-start | bytes 1572872 | tf_op jit(solution)/shard_map/ppermute | solution.py:46
  550.4 116.6 %collective-permute-start.77 = (bf16[128,2048]{1,0:T(8,128)(2,1)}, bf16[128,2048]{1,0:T(8,128)(2,1)}, u32[]{:S(2)}, u32[]{:S(2)}) collective-permute-start(bf16[128,2048]{1,0:T(8,128)(2,1)} %fusion.36), channel_id=1, source_target_pairs={{0,16},{16,0},{8,24},{24,8},{1,17},{17,1},{9,25},{25,9},{2,18},{18... | collective-permute-start | bytes 1572872 | tf_op jit(solution)/shard_map/ppermute | solution.py:46
  627.6 57.7 %collective-permute-start.48 = (bf16[256,1536]{1,0:T(8,128)(2,1)}, bf16[256,1536]{1,0:T(8,128)(2,1)}, u32[]{:S(2)}, u32[]{:S(2)}) collective-permute-start(bf16[256,1536]{1,0:T(8,128)(2,1)} %pad_maximum_fusion.18), channel_id=1, source_target_pairs={{0,16},{16,0},{8,24},{24,8},{1,17},{17,1},{9,25},{25,9},{2,18},{18... | collective-permute-start | bytes 2359304 | tf_op jit(solution)/shard_map/ppermute | solution.py:46
  636.7 24.9 %collective-permute-start.69 = (bf16[128,2048]{1,0:T(8,128)(2,1)}, bf16[128,2048]{1,0:T(8,128)(2,1)}, u32[]{:S(2)}, u32[]{:S(2)}) collective-permute-start(bf16[128,2048]{1,0:T(8,128)(2,1)} %get-tuple-element.117), channel_id=1, source_target_pairs={{0,8},{8,0},{16,24},{24,16},{1,9},{9,1},{17,25},{25,17},{2,10},{10... | collective-permute-start | bytes 1572872 | tf_op jit(solution)/shard_map/ppermute | solution.py:42
  654.6 24.5 %collective-permute-start.46 = (bf16[256,1536]{1,0:T(8,128)(2,1)}, bf16[256,1536]{1,0:T(8,128)(2,1)}, u32[]{:S(2)}, u32[]{:S(2)}) collective-permute-start(bf16[256,1536]{1,0:T(8,128)(2,1)} %pad_maximum_fusion.17), channel_id=1, source_target_pairs={{0,8},{8,0},{16,24},{24,16},{1,9},{9,1},{17,25},{25,17},{2,10},{10... | collective-permute-start | bytes 2359304 | tf_op jit(solution)/shard_map/ppermute | solution.py:42
  661.4 281.6 %reduce-scatter.19.cloned.1.call-start = ((), (), s32[]{:S(2)}) async-start(), calls=%async_computation.13 | async-start | bytes 1310720 | tf_op jit(solution)/shard_map/reduce_scatter | solution.py:101
  667.0 276.6 %reduce-scatter.23.cloned.1.call-start = ((), (), s32[]{:S(2)}) async-start(), calls=%async_computation.15 | async-start | bytes 1310720 | tf_op jit(solution)/shard_map/reduce_scatter | solution.py:101
  692.8 252.6 %reduce-scatter.11.cloned.1.call-start = ((), (), s32[]{:S(2)}) async-start(), calls=%async_computation.9 | async-start | bytes 983040 | tf_op jit(solution)/shard_map/reduce_scatter | solution.py:101
  699.4 39.1 %collective-permute-start.49 = (bf16[128,1536]{1,0:T(8,128)(2,1)}, bf16[128,1536]{1,0:T(8,128)(2,1)S(1)}, u32[]{:S(2)}, u32[]{:S(2)}) collective-permute-start(bf16[128,1536]{1,0:T(8,128)(2,1)} %get-tuple-element.121), channel_id=1, source_target_pairs={{0,8},{8,0},{16,24},{24,16},{1,9},{9,1},{17,25},{25,17},{2,10},{10... | collective-permute-start | bytes 1179656 | tf_op jit(solution)/shard_map/ppermute | solution.py:42
  724.5 62.5 %collective-permute-start.39 = (bf16[592,1024]{1,0:T(8,128)(2,1)}, bf16[592,1024]{1,0:T(8,128)(2,1)}, u32[]{:S(2)}, u32[]{:S(2)}) collective-permute-start(bf16[592,1024]{1,0:T(8,128)(2,1)} %convolution_convert_fusion), channel_id=1, source_target_pairs={{0,4},{4,0},{1,5},{5,1},{2,6},{6,2},{3,7},{7,3},{8,12},{12,8},{9,1... | collective-permute-start | bytes 3637256 | tf_op jit(solution)/shard_map/ppermute | solution.py:50
  725.8 55.5 %collective-permute-start.63 = (bf16[256,2048]{1,0:T(8,128)(2,1)}, bf16[256,2048]{1,0:T(8,128)(2,1)}, u32[]{:S(2)}, u32[]{:S(2)}) collective-permute-start(bf16[256,2048]{1,0:T(8,128)(2,1)} %pad_maximum_fusion.4), channel_id=1, source_target_pairs={{0,16},{16,0},{8,24},{24,8},{1,17},{17,1},{9,25},{25,9},{2,18},{18... | collective-permute-start | bytes 3145736 | tf_op jit(solution)/shard_map/ppermute | solution.py:46
  728.6 26.3 %collective-permute-start.61 = (bf16[256,2048]{1,0:T(8,128)(2,1)}, bf16[256,2048]{1,0:T(8,128)(2,1)}, u32[]{:S(2)}, u32[]{:S(2)}) collective-permute-start(bf16[256,2048]{1,0:T(8,128)(2,1)} %pad_maximum_fusion.3), channel_id=1, source_target_pairs={{0,8},{8,0},{16,24},{24,16},{1,9},{9,1},{17,25},{25,17},{2,10},{10... | collective-permute-start | bytes 3145736 | tf_op jit(solution)/shard_map/ppermute | solution.py:42
  737.2 47.0 %collective-permute-start.73 = (bf16[256,2048]{1,0:T(8,128)(2,1)}, bf16[256,2048]{1,0:T(8,128)(2,1)}, u32[]{:S(2)}, u32[]{:S(2)}) collective-permute-start(bf16[256,2048]{1,0:T(8,128)(2,1)} %pad_maximum_fusion.8), channel_id=1, source_target_pairs={{0,16},{16,0},{8,24},{24,8},{1,17},{17,1},{9,25},{25,9},{2,18},{18... | collective-permute-start | bytes 3145736 | tf_op jit(solution)/shard_map/ppermute | solution.py:46
  738.5 38.1 %collective-permute-start.71 = (bf16[256,2048]{1,0:T(8,128)(2,1)}, bf16[256,2048]{1,0:T(8,128)(2,1)}, u32[]{:S(2)}, u32[]{:S(2)}) collective-permute-start(bf16[256,2048]{1,0:T(8,128)(2,1)} %pad_maximum_fusion.7), channel_id=1, source_target_pairs={{0,8},{8,0},{16,24},{24,16},{1,9},{9,1},{17,25},{25,17},{2,10},{10... | collective-permute-start | bytes 3145736 | tf_op jit(solution)/shard_map/ppermute | solution.py:42
  742.3 205.3 %reduce-scatter.13.cloned.1.call-start = ((), (), s32[]{:S(2)}) async-start(), calls=%async_computation.10 | async-start | bytes 327680 | tf_op jit(solution)/shard_map/reduce_scatter | solution.py:101
  759.2 114.1 %collective-permute-start.62 = (bf16[128,2048]{1,0:T(8,128)(2,1)}, bf16[128,2048]{1,0:T(8,128)(2,1)}, u32[]{:S(2)}, u32[]{:S(2)}) collective-permute-start(bf16[128,2048]{1,0:T(8,128)(2,1)} %fusion.54), channel_id=1, source_target_pairs={{0,16},{16,0},{8,24},{24,8},{1,17},{17,1},{9,25},{25,9},{2,18},{18... | collective-permute-start | bytes 1572872 | tf_op jit(solution)/shard_map/ppermute | solution.py:46
  781.0 55.9 %collective-permute-start.72 = (bf16[128,2048]{1,0:T(8,128)(2,1)}, bf16[128,2048]{1,0:T(8,128)(2,1)}, u32[]{:S(2)}, u32[]{:S(2)}) collective-permute-start(bf16[128,2048]{1,0:T(8,128)(2,1)} %fusion.42), channel_id=1, source_target_pairs={{0,16},{16,0},{8,24},{24,8},{1,17},{17,1},{9,25},{25,9},{2,18},{18... | collective-permute-start | bytes 1572872 | tf_op jit(solution)/shard_map/ppermute | solution.py:46
  833.7 53.7 %collective-permute-start.43 = (bf16[256,1536]{1,0:T(8,128)(2,1)}, bf16[256,1536]{1,0:T(8,128)(2,1)}, u32[]{:S(2)}, u32[]{:S(2)}) collective-permute-start(bf16[256,1536]{1,0:T(8,128)(2,1)} %pad_maximum_fusion.16), channel_id=1, source_target_pairs={{0,16},{16,0},{8,24},{24,8},{1,17},{17,1},{9,25},{25,9},{2,18},{18... | collective-permute-start | bytes 2359304 | tf_op jit(solution)/shard_map/ppermute | solution.py:46
  840.1 24.8 %collective-permute-start.74 = (bf16[128,2048]{1,0:T(8,128)(2,1)}, bf16[128,2048]{1,0:T(8,128)(2,1)}, u32[]{:S(2)}, u32[]{:S(2)}) collective-permute-start(bf16[128,2048]{1,0:T(8,128)(2,1)} %get-tuple-element.111), channel_id=1, source_target_pairs={{0,8},{8,0},{16,24},{24,16},{1,9},{9,1},{17,25},{25,17},{2,10},{10... | collective-permute-start | bytes 1572872 | tf_op jit(solution)/shard_map/ppermute | solution.py:42
  857.2 25.1 %collective-permute-start.41 = (bf16[256,1536]{1,0:T(8,128)(2,1)}, bf16[256,1536]{1,0:T(8,128)(2,1)}, u32[]{:S(2)}, u32[]{:S(2)}) collective-permute-start(bf16[256,1536]{1,0:T(8,128)(2,1)} %pad_maximum_fusion.15), channel_id=1, source_target_pairs={{0,8},{8,0},{16,24},{24,16},{1,9},{9,1},{17,25},{25,17},{2,10},{10... | collective-permute-start | bytes 2359304 | tf_op jit(solution)/shard_map/ppermute | solution.py:42
  864.9 84.2 %reduce-scatter.21.cloned.1.call-start = ((), (), s32[]{:S(2)}) async-start(), calls=%async_computation.14 | async-start | bytes 1310720 | tf_op jit(solution)/shard_map/reduce_scatter | solution.py:101
  873.1 77.9 %reduce-scatter.17.cloned.1.call-start = ((), (), s32[]{:S(2)}) async-start(), calls=%async_computation.12 | async-start | bytes 1310720 | tf_op jit(solution)/shard_map/reduce_scatter | solution.py:101
  894.9 68.2 %reduce-scatter.9.cloned.1.call-start = ((), (), s32[]{:S(2)}) async-start(), calls=%async_computation.8 | async-start | bytes 983040 | tf_op jit(solution)/shard_map/reduce_scatter | solution.py:101
  917.1 102.2 %all-gather.31.cloned.1.call-start = ((), (), s32[]{:S(2)}) async-start(), calls=%async_computation.21 | async-start | bytes 3276800 | tf_op jit(solution)/shard_map/all_gather | solution.py:289
  940.5 133.9 %all-gather.29.cloned.1.call-start = ((), (), s32[]{:S(2)}) async-start(), calls=%async_computation.20 | async-start | bytes 3276800 | tf_op jit(solution)/shard_map/all_gather | solution.py:289
  941.0 192.9 %all-gather.33.cloned.1.call-start = ((), (), s32[]{:S(2)}) async-start(), calls=%async_computation.22 | async-start | bytes 2703360 | tf_op jit(solution)/shard_map/all_gather | solution.py:317
  (164 other events, 1939.1 us)
Sparse Core Ops, SparseCore 0:
  10.2 36.8 all-gather.22
  49.2 35.7 all-gather.20
  87.1 36.2 all-gather.24
  124.8 30.8 all-gather.26
  661.5 19.2 reduce-scatter.14
  683.0 25.3 reduce-scatter.18
  710.7 25.7 reduce-scatter.22
  742.4 22.9 reduce-scatter.10
  865.0 17.0 reduce-scatter.12
  884.2 25.3 reduce-scatter.20
  912.6 25.8 reduce-scatter.16
  941.1 21.9 reduce-scatter.8
  965.3 54.0 all-gather.30
  1020.8 53.5 all-gather.28
  1077.1 56.8 all-gather.32
